TPU v7x, 128 devices: a whole 4x4x4 slice. The times are simulated.
128 devices in a mesh: leaf: 32 (over y, z, core), sub: 4 (over x).
Axes of the slice: x: 4, y: 4, z: 4, core: 2. Of those that a mesh axis runs over, the one named last changes fastest.
Arguments:
- probe: bfloat16 [8192, 16, 256], P(('leaf', 'sub')), may hold values from -6 to 6
- weights: bfloat16 [8192, 16, 256], P(('leaf', 'sub')), may hold values from -6 to 6
- points: bfloat16 [8192, 3, 256], P(('leaf', 'sub')), may hold values from -3 to 3
- skeleton: bfloat16 [8192, 192], P(('leaf', 'sub')), may hold values from -3 to 3
- row_basis: bfloat16 [8192, 64, 256], P(('leaf', 'sub')), may hold values from -0.75 to 0.75
- col_basis: bfloat16 [8192, 64, 256], P(('leaf', 'sub')), may hold values from -0.375 to 0.375
- near_leaf: int32 [8192, 12], P(('leaf', 'sub')), may hold values from 0 to 8191, as said below
- far_slot: int32 [8192, 64], P(('leaf', 'sub')), may hold values from 0 to 511, as said below
- send_leaf: int32 [128, 128, 4], P(('leaf', 'sub')), may hold values from 0 to 63, as said below
Outputs:
- product: float32 [8192, 16, 256], P(('leaf', 'sub'))
- adjoint: float32 [8192, 16, 256], P(('leaf', 'sub'))
Inputs may be any that keep to these rules, and one draw needn't show every extreme that they name: `near_leaf`: entry 0 of a leaf's list is the leaf itself; every entry lies within 8 leaves of it in the global order. `far_slot`: A slot s stands for slot s % 4 of what device s // 4 of leaf+sub sends to the leaf's device. `send_leaf`: leaves are counted within the sending device; for one sender and one receiver the 4 entries differ.
All inputs are finite; a program needn't handle non-finite values.
Results may differ from a plain program's by a relative error of at most 0.0085.
Values may be sent and summed in bfloat16 or wider, within the bound.
A program may use at most 256 MiB of HBM per device.

v0:
```python
import jax
import jax.numpy as jnp
from jax import lax
from jax.sharding import PartitionSpec as P

NEAR_REACH = 8


AMPLITUDE = 0.5
LENGTH_SCALE = 0.5
SOFTENING = 0.01
NUGGET = 0.5


def padded(block, sides, width):
    for axis, dim in sides:
        count = lax.axis_size(axis)
        forward = [(i, i + 1) for i in range(count - 1)]
        backward = [(target, source) for source, target in forward]
        low = lax.ppermute(
            lax.slice_in_dim(block, block.shape[dim] - width, None, axis=dim), axis, forward
        )
        high = lax.ppermute(lax.slice_in_dim(block, 0, width, axis=dim), axis, backward)
        block = jnp.concatenate([low, block, high], axis=dim)
    return block


def matern(distance_sq):
    scaled = jnp.sqrt(distance_sq + SOFTENING) * (3.0**0.5 / LENGTH_SCALE)
    return AMPLITUDE * (1.0 + scaled) * jnp.exp(-scaled)


def sq_dist(left_xyz, right_xyz):
    total = jnp.zeros(left_xyz.shape[:-2] + (left_xyz.shape[-1], right_xyz.shape[-1]), jnp.float32)
    for comp in range(3):
        offset_comp = left_xyz[..., comp, :, None] - right_xyz[..., comp, None, :]
        total = total + offset_comp * offset_comp
    return total


def near_pass(
    src_xyz,
    src_weights,
    src_glob,
    lists,
    ext_xyz,
    ext_probe,
    first_glob,
    block_rows,
    reach,
    src_shift,
):
    source_count, rhs_count, leaf_size = src_weights.shape
    extent = ext_xyz.shape[0]
    identity_mat = jnp.eye(leaf_size, dtype=jnp.float32)
    window_len = block_rows + 2 * reach

    def group_step(padded_acc, begin_row):
        own_xyz = lax.dynamic_slice_in_dim(src_xyz, begin_row, block_rows, 0).astype(jnp.float32)
        own_w = lax.dynamic_slice_in_dim(src_weights, begin_row, block_rows, 0)
        own_glob = lax.dynamic_slice_in_dim(src_glob, begin_row, block_rows, 0)
        near_ids = lax.dynamic_slice_in_dim(lists, begin_row, block_rows, 0)
        relative_raw = near_ids - first_glob
        relative = jnp.clip(relative_raw, 0, extent - 1)
        target_xyz = ext_xyz[relative].astype(jnp.float32)
        target_probe = ext_probe[relative]
        kernel = matern(sq_dist(own_xyz[:, None], target_xyz))
        self_mask = (near_ids == own_glob[:, None]).astype(jnp.float32)
        kernel = (kernel + NUGGET * self_mask[:, :, None, None] * identity_mat).astype(jnp.bfloat16)
        forward = jnp.einsum(
            "gmab,gmrb->gra", kernel, target_probe, preferred_element_type=jnp.float32
        )
        pushed = jnp.einsum("gmab,gra->gmrb", kernel, own_w, preferred_element_type=jnp.float32)
        window_start = begin_row + src_shift
        local_pos = relative_raw + reach - window_start
        window = lax.dynamic_slice_in_dim(padded_acc, window_start, window_len, 0)
        window = window.at[local_pos.reshape(-1)].add(pushed.reshape(-1, rhs_count, leaf_size))
        padded_acc = lax.dynamic_update_slice_in_dim(padded_acc, window, window_start, 0)
        return (padded_acc, forward)

    begins = jnp.arange(0, source_count, block_rows, dtype=jnp.int32)
    initial = jnp.zeros((extent + 2 * reach, rhs_count, leaf_size), jnp.float32)
    padded_acc, forward = lax.scan(group_step, initial, begins)
    adjoint_ext = padded_acc[reach : reach + extent]
    return (forward.reshape(source_count, rhs_count, leaf_size), adjoint_ext)


def local(probe, weights, points, skeleton, row_basis, col_basis, near_leaf, far_slot, send_leaf):
    leaf_count, rhs_count, leaf_size = probe.shape
    rank_size = row_basis.shape[1]
    device_total = lax.axis_size(("leaf", "sub"))
    first_leaf = lax.axis_index(("leaf", "sub")) * leaf_count
    rim_width = NEAR_REACH
    block_rows = 1
    for candidate in (2, 4, 8):
        block_rows = candidate
    own_glob = first_leaf + jnp.arange(leaf_count, dtype=jnp.int32)
    coef = jnp.einsum("lka,lra->lkr", col_basis, probe, preferred_element_type=jnp.float32).astype(
        jnp.bfloat16
    )
    back_coef = jnp.einsum(
        "lka,lra->lkr", row_basis, weights, preferred_element_type=jnp.float32
    ).astype(jnp.bfloat16)
    routes = send_leaf[0]
    slot_cap = routes.shape[1]
    coef_width = rank_size * rhs_count
    payload = jnp.concatenate([coef.reshape(leaf_count, coef_width), skeleton], axis=1)
    outgoing = payload[routes]
    arrived = lax.all_to_all(outgoing, ("leaf", "sub"), split_axis=0, concat_axis=0, tiled=True)
    arrived = arrived.reshape(device_total * slot_cap, payload.shape[1])
    first_glob = first_leaf - rim_width
    stacked = jnp.concatenate([points, probe], axis=1)
    ext_rows = padded(stacked, ((("leaf", "sub"), 0),), rim_width)
    near_forward, adjoint_ext = near_pass(
        points,
        weights,
        own_glob,
        near_leaf,
        ext_rows[:, :3],
        ext_rows[:, 3:],
        first_glob,
        block_rows,
        rim_width,
        rim_width,
    )
    rims = jnp.concatenate([adjoint_ext[:rim_width], adjoint_ext[leaf_count + rim_width :]], axis=0)
    arrived_rims = padded(rims.astype(jnp.bfloat16), ((("leaf", "sub"), 0),), rim_width).astype(
        rims.dtype
    )
    near_adjoint = adjoint_ext[rim_width : rim_width + leaf_count]
    near_adjoint = near_adjoint.at[:rim_width].add(arrived_rims[:rim_width])
    near_adjoint = near_adjoint.at[leaf_count - rim_width :].add(arrived_rims[3 * rim_width :])
    far_count = far_slot.shape[1]
    remote = arrived[far_slot]
    remote_coef = remote[:, :, :coef_width].reshape(leaf_count, far_count, rank_size, rhs_count)
    remote_skel = remote[:, :, coef_width:].reshape(leaf_count, far_count, 3, rank_size)
    own_skel = skeleton.reshape(leaf_count, 3, rank_size)
    far_rows = min(leaf_count, 32)
    while leaf_count % far_rows != 0:
        far_rows = far_rows // 2

    def far_step(begin_row):
        skel_own = lax.dynamic_slice_in_dim(own_skel, begin_row, far_rows, 0).astype(jnp.float32)
        skel_far = lax.dynamic_slice_in_dim(remote_skel, begin_row, far_rows, 0).astype(jnp.float32)
        coef_far = lax.dynamic_slice_in_dim(remote_coef, begin_row, far_rows, 0)
        back_own = lax.dynamic_slice_in_dim(back_coef, begin_row, far_rows, 0)
        coupling = matern(sq_dist(skel_own[:, None], skel_far)).astype(jnp.bfloat16)
        gathered = jnp.einsum(
            "gmkl,gmlr->gkr", coupling, coef_far, preferred_element_type=jnp.float32
        ).astype(jnp.bfloat16)
        returned = jnp.einsum(
            "gmkl,gkr->gmlr", coupling, back_own, preferred_element_type=jnp.float32
        )
        return (gathered, returned)

    far_begins = jnp.arange(0, leaf_count, far_rows, dtype=jnp.int32)
    far_in, returned = lax.map(far_step, far_begins)
    far_in = far_in.reshape(leaf_count, rank_size, rhs_count)
    slot_sums = jax.ops.segment_sum(
        returned.reshape(leaf_count * far_count, coef_width),
        far_slot.reshape(-1),
        num_segments=device_total * slot_cap,
    )
    came_back = lax.all_to_all(
        slot_sums.reshape(device_total, slot_cap, coef_width).astype(jnp.bfloat16),
        ("leaf", "sub"),
        split_axis=0,
        concat_axis=0,
        tiled=True,
    ).astype(jnp.float32)
    came_back = came_back.reshape(device_total * slot_cap, coef_width)
    high_part = came_back.astype(jnp.bfloat16)
    low_part = (came_back - high_part.astype(jnp.float32)).astype(jnp.bfloat16)
    both_parts = jnp.concatenate([high_part, low_part], axis=1)
    leaf_ids = jnp.arange(leaf_count, dtype=jnp.int32)
    owner_hot = (leaf_ids[:, None] == routes.reshape(-1)[None, :]).astype(jnp.bfloat16)
    owner_sums = jnp.dot(owner_hot, both_parts, preferred_element_type=jnp.float32)
    far_returned = owner_sums[:, :coef_width] + owner_sums[:, coef_width:]
    far_returned = far_returned.astype(jnp.bfloat16).reshape(leaf_count, rank_size, rhs_count)
    product = near_forward + jnp.einsum(
        "lkr,lka->lra", far_in, row_basis, preferred_element_type=jnp.float32
    )
    adjoint = near_adjoint + jnp.einsum(
        "lkr,lka->lra", far_returned, col_basis, preferred_element_type=jnp.float32
    )
    return (product, adjoint)


def solution(mesh):
    in_specs = (
        P(("leaf", "sub"), None, None),
        P(("leaf", "sub"), None, None),
        P(("leaf", "sub"), None, None),
        P(("leaf", "sub"), None),
        P(("leaf", "sub"), None, None),
        P(("leaf", "sub"), None, None),
        P(("leaf", "sub"), None),
        P(("leaf", "sub"), None),
        P(("leaf", "sub"), None, None),
    )
    out_specs = (P(("leaf", "sub"), None, None), P(("leaf", "sub"), None, None))
    return jax.shard_map(local, mesh=mesh, in_specs=in_specs, out_specs=out_specs, check_vma=False)
```

profile of v0, /device:TPU:1, one launch (start us, length us, event | category | flops | bytes accessed | tf_op | source)
XLA Modules:
  0.0 1183.3 jit_solution(565518432272864698)
XLA Ops:
  23.7 10.0 all-to-all-start
  47.1 585.1 %while.30 = (s32[]{:T(128)}, f32[96,16,256]{2,1,0:T(8,128)}, f32[8,8,16,256]{3,2,1,0:T(8,128)}, s32[8]{0:T(128)}, s32[64,12]{1,0:T(8,128)}, /*index=5*/s32[]{:T(...) while((s32[]{:T(128)}, f32[96,16,256]{2,1,0:T(8,128)}, ...), condition=%wide.region_2.3_spmd.clone, body=%wide.region_0.2_spmd.clone.sunk | while | flops 617169024 | bytes 16810464 | solution.py:83
  60.4 24.9 %fusion.78 = f32[8,8,16,256]{3,2,1,0:T(8,128)} fusion(f32[8,8,16,256]{3,2,1,0:T(8,128)} %get-tuple-element.571, s32[]{:T(128)S(6)} %copy.153, bf16[8,12,16,256]{3,2,1,0:T(8,128)(2,1)} %bitcast.140, f32[256,256]{1,0:T(8,128)S(1)} %fusion.76, f32[8,12]{1,0:T(8,128)S(1)} %compare_select_fusion.8, f32[8,12,256]{2,1,0:T(8,128)} %get-tuple-element.547, ...), kind=kOutput, calls=%fused_computation.40.clone.1 | convolution fusion | flops 308281344 | bytes 1565060 | tf_op jit(solution)/shard_map/while/body/eval_jaxpr/gmab,gmrb->gra/dot_general | solution.py:70
  85.3 24.2 %fusion.77 = f32[8,16,12,256]{3,1,2,0:T(8,128)} fusion(f32[256,256]{1,0:T(8,128)} %copy-done.6, f32[8,12]{1,0:T(8,128)S(1)} %compare_select_fusion.8, f32[8,12,256]{2,1,0:T(8,128)S(1)} %copy-done.7, f32[8,256]{1,0:T(8,128)S(1)} %copy-done.11, f32[8,12,256]{2,1,0:T(8,128)S(1)} %copy-done.8, f32[8,256]{1,0:T(8,128)S(1)} %copy-done.12, ...), kind=kOutput, calls=%fused_computation.38.clone.1 | convolution fusion | flops 308281344 | bytes 2220420 | tf_op jit(solution)/shard_map/while/body/eval_jaxpr/gmab,gra->gmrb/dot_general | solution.py:73
  109.5 8.9 scatter_fusion
  132.2 24.9 %fusion.78 = f32[8,8,16,256]{3,2,1,0:T(8,128)} fusion(f32[8,8,16,256]{3,2,1,0:T(8,128)} %get-tuple-element.571, s32[]{:T(128)S(6)} %copy.153, bf16[8,12,16,256]{3,2,1,0:T(8,128)(2,1)} %bitcast.140, f32[256,256]{1,0:T(8,128)S(1)} %fusion.76, f32[8,12]{1,0:T(8,128)S(1)} %compare_select_fusion.8, f32[8,12,256]{2,1,0:T(8,128)} %get-tuple-element.547, ...), kind=kOutput, calls=%fused_computation.40.clone.1 | convolution fusion | flops 308281344 | bytes 1565060 | tf_op jit(solution)/shard_map/while/body/eval_jaxpr/gmab,gmrb->gra/dot_general | solution.py:70
  157.1 24.2 %fusion.77 = f32[8,16,12,256]{3,1,2,0:T(8,128)} fusion(f32[256,256]{1,0:T(8,128)} %copy-done.6, f32[8,12]{1,0:T(8,128)S(1)} %compare_select_fusion.8, f32[8,12,256]{2,1,0:T(8,128)S(1)} %copy-done.7, f32[8,256]{1,0:T(8,128)S(1)} %copy-done.11, f32[8,12,256]{2,1,0:T(8,128)S(1)} %copy-done.8, f32[8,256]{1,0:T(8,128)S(1)} %copy-done.12, ...), kind=kOutput, calls=%fused_computation.38.clone.1 | convolution fusion | flops 308281344 | bytes 2220420 | tf_op jit(solution)/shard_map/while/body/eval_jaxpr/gmab,gra->gmrb/dot_general | solution.py:73
  181.2 8.9 scatter_fusion
  203.9 24.9 %fusion.78 = f32[8,8,16,256]{3,2,1,0:T(8,128)} fusion(f32[8,8,16,256]{3,2,1,0:T(8,128)} %get-tuple-element.571, s32[]{:T(128)S(6)} %copy.153, bf16[8,12,16,256]{3,2,1,0:T(8,128)(2,1)} %bitcast.140, f32[256,256]{1,0:T(8,128)S(1)} %fusion.76, f32[8,12]{1,0:T(8,128)S(1)} %compare_select_fusion.8, f32[8,12,256]{2,1,0:T(8,128)} %get-tuple-element.547, ...), kind=kOutput, calls=%fused_computation.40.clone.1 | convolution fusion | flops 308281344 | bytes 1565060 | tf_op jit(solution)/shard_map/while/body/eval_jaxpr/gmab,gmrb->gra/dot_general | solution.py:70
  228.8 24.2 %fusion.77 = f32[8,16,12,256]{3,1,2,0:T(8,128)} fusion(f32[256,256]{1,0:T(8,128)} %copy-done.6, f32[8,12]{1,0:T(8,128)S(1)} %compare_select_fusion.8, f32[8,12,256]{2,1,0:T(8,128)S(1)} %copy-done.7, f32[8,256]{1,0:T(8,128)S(1)} %copy-done.11, f32[8,12,256]{2,1,0:T(8,128)S(1)} %copy-done.8, f32[8,256]{1,0:T(8,128)S(1)} %copy-done.12, ...), kind=kOutput, calls=%fused_computation.38.clone.1 | convolution fusion | flops 308281344 | bytes 2220420 | tf_op jit(solution)/shard_map/while/body/eval_jaxpr/gmab,gra->gmrb/dot_general | solution.py:73
  253.0 8.9 scatter_fusion
  275.7 24.9 %fusion.78 = f32[8,8,16,256]{3,2,1,0:T(8,128)} fusion(f32[8,8,16,256]{3,2,1,0:T(8,128)} %get-tuple-element.571, s32[]{:T(128)S(6)} %copy.153, bf16[8,12,16,256]{3,2,1,0:T(8,128)(2,1)} %bitcast.140, f32[256,256]{1,0:T(8,128)S(1)} %fusion.76, f32[8,12]{1,0:T(8,128)S(1)} %compare_select_fusion.8, f32[8,12,256]{2,1,0:T(8,128)} %get-tuple-element.547, ...), kind=kOutput, calls=%fused_computation.40.clone.1 | convolution fusion | flops 308281344 | bytes 1565060 | tf_op jit(solution)/shard_map/while/body/eval_jaxpr/gmab,gmrb->gra/dot_general | solution.py:70
  300.6 24.2 %fusion.77 = f32[8,16,12,256]{3,1,2,0:T(8,128)} fusion(f32[256,256]{1,0:T(8,128)} %copy-done.6, f32[8,12]{1,0:T(8,128)S(1)} %compare_select_fusion.8, f32[8,12,256]{2,1,0:T(8,128)S(1)} %copy-done.7, f32[8,256]{1,0:T(8,128)S(1)} %copy-done.11, f32[8,12,256]{2,1,0:T(8,128)S(1)} %copy-done.8, f32[8,256]{1,0:T(8,128)S(1)} %copy-done.12, ...), kind=kOutput, calls=%fused_computation.38.clone.1 | convolution fusion | flops 308281344 | bytes 2220420 | tf_op jit(solution)/shard_map/while/body/eval_jaxpr/gmab,gra->gmrb/dot_general | solution.py:73
  324.8 8.9 scatter_fusion
  347.4 24.9 %fusion.78 = f32[8,8,16,256]{3,2,1,0:T(8,128)} fusion(f32[8,8,16,256]{3,2,1,0:T(8,128)} %get-tuple-element.571, s32[]{:T(128)S(6)} %copy.153, bf16[8,12,16,256]{3,2,1,0:T(8,128)(2,1)} %bitcast.140, f32[256,256]{1,0:T(8,128)S(1)} %fusion.76, f32[8,12]{1,0:T(8,128)S(1)} %compare_select_fusion.8, f32[8,12,256]{2,1,0:T(8,128)} %get-tuple-element.547, ...), kind=kOutput, calls=%fused_computation.40.clone.1 | convolution fusion | flops 308281344 | bytes 1565060 | tf_op jit(solution)/shard_map/while/body/eval_jaxpr/gmab,gmrb->gra/dot_general | solution.py:70
  372.3 24.2 %fusion.77 = f32[8,16,12,256]{3,1,2,0:T(8,128)} fusion(f32[256,256]{1,0:T(8,128)} %copy-done.6, f32[8,12]{1,0:T(8,128)S(1)} %compare_select_fusion.8, f32[8,12,256]{2,1,0:T(8,128)S(1)} %copy-done.7, f32[8,256]{1,0:T(8,128)S(1)} %copy-done.11, f32[8,12,256]{2,1,0:T(8,128)S(1)} %copy-done.8, f32[8,256]{1,0:T(8,128)S(1)} %copy-done.12, ...), kind=kOutput, calls=%fused_computation.38.clone.1 | convolution fusion | flops 308281344 | bytes 2220420 | tf_op jit(solution)/shard_map/while/body/eval_jaxpr/gmab,gra->gmrb/dot_general | solution.py:73
  396.5 8.9 scatter_fusion
  419.2 24.9 %fusion.78 = f32[8,8,16,256]{3,2,1,0:T(8,128)} fusion(f32[8,8,16,256]{3,2,1,0:T(8,128)} %get-tuple-element.571, s32[]{:T(128)S(6)} %copy.153, bf16[8,12,16,256]{3,2,1,0:T(8,128)(2,1)} %bitcast.140, f32[256,256]{1,0:T(8,128)S(1)} %fusion.76, f32[8,12]{1,0:T(8,128)S(1)} %compare_select_fusion.8, f32[8,12,256]{2,1,0:T(8,128)} %get-tuple-element.547, ...), kind=kOutput, calls=%fused_computation.40.clone.1 | convolution fusion | flops 308281344 | bytes 1565060 | tf_op jit(solution)/shard_map/while/body/eval_jaxpr/gmab,gmrb->gra/dot_general | solution.py:70
  444.1 24.2 %fusion.77 = f32[8,16,12,256]{3,1,2,0:T(8,128)} fusion(f32[256,256]{1,0:T(8,128)} %copy-done.6, f32[8,12]{1,0:T(8,128)S(1)} %compare_select_fusion.8, f32[8,12,256]{2,1,0:T(8,128)S(1)} %copy-done.7, f32[8,256]{1,0:T(8,128)S(1)} %copy-done.11, f32[8,12,256]{2,1,0:T(8,128)S(1)} %copy-done.8, f32[8,256]{1,0:T(8,128)S(1)} %copy-done.12, ...), kind=kOutput, calls=%fused_computation.38.clone.1 | convolution fusion | flops 308281344 | bytes 2220420 | tf_op jit(solution)/shard_map/while/body/eval_jaxpr/gmab,gra->gmrb/dot_general | solution.py:73
  468.2 8.9 scatter_fusion
  490.9 24.9 %fusion.78 = f32[8,8,16,256]{3,2,1,0:T(8,128)} fusion(f32[8,8,16,256]{3,2,1,0:T(8,128)} %get-tuple-element.571, s32[]{:T(128)S(6)} %copy.153, bf16[8,12,16,256]{3,2,1,0:T(8,128)(2,1)} %bitcast.140, f32[256,256]{1,0:T(8,128)S(1)} %fusion.76, f32[8,12]{1,0:T(8,128)S(1)} %compare_select_fusion.8, f32[8,12,256]{2,1,0:T(8,128)} %get-tuple-element.547, ...), kind=kOutput, calls=%fused_computation.40.clone.1 | convolution fusion | flops 308281344 | bytes 1565060 | tf_op jit(solution)/shard_map/while/body/eval_jaxpr/gmab,gmrb->gra/dot_general | solution.py:70
  515.8 24.2 %fusion.77 = f32[8,16,12,256]{3,1,2,0:T(8,128)} fusion(f32[256,256]{1,0:T(8,128)} %copy-done.6, f32[8,12]{1,0:T(8,128)S(1)} %compare_select_fusion.8, f32[8,12,256]{2,1,0:T(8,128)S(1)} %copy-done.7, f32[8,256]{1,0:T(8,128)S(1)} %copy-done.11, f32[8,12,256]{2,1,0:T(8,128)S(1)} %copy-done.8, f32[8,256]{1,0:T(8,128)S(1)} %copy-done.12, ...), kind=kOutput, calls=%fused_computation.38.clone.1 | convolution fusion | flops 308281344 | bytes 2220420 | tf_op jit(solution)/shard_map/while/body/eval_jaxpr/gmab,gra->gmrb/dot_general | solution.py:73
  540.0 8.9 scatter_fusion
  562.6 24.9 %fusion.78 = f32[8,8,16,256]{3,2,1,0:T(8,128)} fusion(f32[8,8,16,256]{3,2,1,0:T(8,128)} %get-tuple-element.571, s32[]{:T(128)S(6)} %copy.153, bf16[8,12,16,256]{3,2,1,0:T(8,128)(2,1)} %bitcast.140, f32[256,256]{1,0:T(8,128)S(1)} %fusion.76, f32[8,12]{1,0:T(8,128)S(1)} %compare_select_fusion.8, f32[8,12,256]{2,1,0:T(8,128)} %get-tuple-element.547, ...), kind=kOutput, calls=%fused_computation.40.clone.1 | convolution fusion | flops 308281344 | bytes 1565060 | tf_op jit(solution)/shard_map/while/body/eval_jaxpr/gmab,gmrb->gra/dot_general | solution.py:70
  587.5 24.2 %fusion.77 = f32[8,16,12,256]{3,1,2,0:T(8,128)} fusion(f32[256,256]{1,0:T(8,128)} %copy-done.6, f32[8,12]{1,0:T(8,128)S(1)} %compare_select_fusion.8, f32[8,12,256]{2,1,0:T(8,128)S(1)} %copy-done.7, f32[8,256]{1,0:T(8,128)S(1)} %copy-done.11, f32[8,12,256]{2,1,0:T(8,128)S(1)} %copy-done.8, f32[8,256]{1,0:T(8,128)S(1)} %copy-done.12, ...), kind=kOutput, calls=%fused_computation.38.clone.1 | convolution fusion | flops 308281344 | bytes 2220420 | tf_op jit(solution)/shard_map/while/body/eval_jaxpr/gmab,gra->gmrb/dot_general | solution.py:73
  611.7 8.9 scatter_fusion
  637.1 19.8 %gather_fusion.3 = bf16[4096,1216]{1,0:T(8,128)(2,1)} fusion(bf16[512,1216]{1,0:T(8,128)(2,1)S(1)} %reshape.185, s32[4096]{0:T(1024)} %broadcast_clamp_fusion), kind=kCustom, calls=%fused_computation.3 | custom fusion | bytes 19939328 | tf_op jit(solution)/shard_map/gather | solution.py:134
  660.1 8.4 slice.192
  668.6 4.5 copy.134
  673.1 15.6 %copy.135 = bf16[64,64,1024]{1,2,0:T(8,128)(2,1)} copy(bf16[64,64,1024]{2,1,0:T(8,128)(2,1)} %slice.192) | data formatting | bytes 16777216
  688.7 367.7 %while.29 = (s32[]{:T(128)}, bf16[2,32,64,16]{2,3,1,0:T(8,128)(2,1)S(1)}, f32[2,32,64,64,16]{2,1,0,4,3:T(8,128)}, s32[2]{0:T(128)S(1)}, bf16[64,3,64]{2,0,1:T(8,...) while((s32[]{:T(128)}, ...), condition=%wide.region_4.5_spmd, body=%wide.region_3.4_spmd.sunk | while | flops 788961280 | bytes 98750808 | solution.py:157
  700.6 9.0 constant_dynamic-slice_fusion.6
  709.6 15.3 %copy.141 = bf16[32,64,64,16]{2,3,1,0:T(8,128)(2,1)} copy(bf16[32,64,64,16]{1,3,2,0:T(8,128)(2,1)} %constant_dynamic-slice_fusion.6) | data formatting | bytes 8388608 | tf_op jit(solution)/shard_map/while/body/eval_jaxpr/dynamic_slice | solution.py:145
  725.0 60.4 %fusion.71 = bf16[2,32,64,16]{2,3,1,0:T(8,128)(2,1)S(1)} fusion(bf16[2,32,64,16]{2,3,1,0:T(8,128)(2,1)S(1)} %get-tuple-element.613, s32[]{:T(128)S(6)} %copy.162, bf16[32,64,64,16]{2,3,1,0:T(8,128)(2,1)} %copy.141, f32[32,64,64]{2,1,0:T(8,128)} %get-tuple-element.528, f32[32,64]{1,0:T(8,128)S(1)} %get-tuple-element.529, ...), kind=kOutput, calls=%fused_computation.14.clone.1 | convolution fusion | flops 394297344 | bytes 6471684 | tf_op jit(solution)/shard_map/while/body/eval_jaxpr/gmkl,gmlr->gkr/dot_general | solution.py:148
  785.4 56.4 %fusion.72 = f32[1,32,64,64,16]{3,4,2,1,0:T(8,128)} fusion(f32[32,64,64]{2,1,0:T(8,128)S(1)} %copy-done.1, f32[32,64]{1,0:T(8,128)S(1)} %get-tuple-element.529, f32[32,64,64]{2,1,0:T(8,128)S(1)} %copy-done.2, f32[32,64]{1,0:T(8,128)S(1)} %get-tuple-element.531, f32[32,64,64]{2,1,0:T(8,128)S(1)} %get-tuple-element.532, ...), kind=kOutput, calls=%fused_computation.10.clone.1 | convolution fusion | flops 394264576 | bytes 11714564 | tf_op jit(solution)/shard_map/while/body/eval_jaxpr/gmkl,gkr->gmlr/dot_general | solution.py:151
  841.8 18.8 %copy.143 = f32[1,32,64,64,16]{2,1,0,4,3:T(8,128)} copy(f32[1,32,64,64,16]{3,4,2,1,0:T(8,128)} %fusion.72) | data formatting | bytes 16777216 | tf_op jit(solution)/shard_map/while/body/jit(dynamic_update_index_in_dim)/dynamic_update_slice | solution.py:157
  860.6 11.9 %constant_dynamic-update-slice_fusion.4 = f32[2,32,64,64,16]{2,1,0,4,3:T(8,128)} fusion(f32[2,32,64,64,16]{2,1,0,4,3:T(8,128)} %get-tuple-element.614, f32[1,32,64,64,16]{2,1,0,4,3:T(8,128)} %copy.143, s32[]{:T(128)S(6)} %copy.162), kind=kLoop, calls=%fused_computation.24.clone.1 | loop fusion | bytes 33554436 | tf_op jit(solution)/shard_map/while/body/jit(dynamic_update_index_in_dim)/dynamic_update_slice | solution.py:157
  884.5 9.0 constant_dynamic-slice_fusion.6
  893.5 15.3 %copy.141 = bf16[32,64,64,16]{2,3,1,0:T(8,128)(2,1)} copy(bf16[32,64,64,16]{1,3,2,0:T(8,128)(2,1)} %constant_dynamic-slice_fusion.6) | data formatting | bytes 8388608 | tf_op jit(solution)/shard_map/while/body/eval_jaxpr/dynamic_slice | solution.py:145
  908.8 60.4 %fusion.71 = bf16[2,32,64,16]{2,3,1,0:T(8,128)(2,1)S(1)} fusion(bf16[2,32,64,16]{2,3,1,0:T(8,128)(2,1)S(1)} %get-tuple-element.613, s32[]{:T(128)S(6)} %copy.162, bf16[32,64,64,16]{2,3,1,0:T(8,128)(2,1)} %copy.141, f32[32,64,64]{2,1,0:T(8,128)} %get-tuple-element.528, f32[32,64]{1,0:T(8,128)S(1)} %get-tuple-element.529, ...), kind=kOutput, calls=%fused_computation.14.clone.1 | convolution fusion | flops 394297344 | bytes 6471684 | tf_op jit(solution)/shard_map/while/body/eval_jaxpr/gmkl,gmlr->gkr/dot_general | solution.py:148
  969.3 56.4 %fusion.72 = f32[1,32,64,64,16]{3,4,2,1,0:T(8,128)} fusion(f32[32,64,64]{2,1,0:T(8,128)S(1)} %copy-done.1, f32[32,64]{1,0:T(8,128)S(1)} %get-tuple-element.529, f32[32,64,64]{2,1,0:T(8,128)S(1)} %copy-done.2, f32[32,64]{1,0:T(8,128)S(1)} %get-tuple-element.531, f32[32,64,64]{2,1,0:T(8,128)S(1)} %get-tuple-element.532, ...), kind=kOutput, calls=%fused_computation.10.clone.1 | convolution fusion | flops 394264576 | bytes 11714564 | tf_op jit(solution)/shard_map/while/body/eval_jaxpr/gmkl,gkr->gmlr/dot_general | solution.py:151
  1025.7 18.8 %copy.143 = f32[1,32,64,64,16]{2,1,0,4,3:T(8,128)} copy(f32[1,32,64,64,16]{3,4,2,1,0:T(8,128)} %fusion.72) | data formatting | bytes 16777216 | tf_op jit(solution)/shard_map/while/body/jit(dynamic_update_index_in_dim)/dynamic_update_slice | solution.py:157
  1044.5 11.9 %constant_dynamic-update-slice_fusion.4 = f32[2,32,64,64,16]{2,1,0,4,3:T(8,128)} fusion(f32[2,32,64,64,16]{2,1,0,4,3:T(8,128)} %get-tuple-element.614, f32[1,32,64,64,16]{2,1,0,4,3:T(8,128)} %copy.143, s32[]{:T(128)S(6)} %copy.162), kind=kLoop, calls=%fused_computation.24.clone.1 | loop fusion | bytes 33554436 | tf_op jit(solution)/shard_map/while/body/jit(dynamic_update_index_in_dim)/dynamic_update_slice | solution.py:157
  1056.4 27.9 %reshape.239 = f32[4096,1024]{0,1:T(8,128)} reshape(f32[2,32,64,64,16]{2,1,0,4,3:T(8,128)} %get-tuple-element.644) | data formatting | bytes 33554432 | tf_op jit(solution)/shard_map/reshape | solution.py:160
  1084.3 17.5 %copy.120 = f32[4096,1024]{1,0:T(8,128)} copy(f32[4096,1024]{0,1:T(8,128)} %reshape.239) | data formatting | bytes 33554432 | tf_op jit(solution)/shard_map/reshape | solution.py:160
  1101.8 37.7 %scatter_custom_fusion.1 = f32[512,1024]{1,0:T(8,128)} fusion(s32[4096]{0:T(1024)} %reshape.237, f32[4096,1024]{1,0:T(8,128)} %copy.120, f32[]{:T(128)} %constant.173.clone.1), kind=kCustom, calls=%fused_computation.79 | custom fusion | flops 4194304 | bytes 2097664 | tf_op jit(solution)/shard_map/scatter-add | solution.py:159
  1142.5 10.2 all-to-all-start.1
  1161.9 6.3 collective-permute-done.2
  (369 shorter events, 175.1 us)
Async XLA Ops:
  0.6 40.0 %copy-start = (bf16[64,64,256]{2,1,0:T(8,128)(2,1)S(1)}, bf16[64,64,256]{2,1,0:T(8,128)(2,1)}, u32[]{:S(2)}) copy-start(bf16[64,64,256]{2,1,0:T(8,128)(2,1)} %param.21) | copy-start | bytes 6291460
  0.6 42.9 %copy-start.3 = (bf16[64,16,256]{2,1,0:T(8,128)(2,1)S(1)}, bf16[64,16,256]{2,1,0:T(8,128)(2,1)}, u32[]{:S(2)}) copy-start(bf16[64,16,256]{2,1,0:T(8,128)(2,1)} %param.17) | copy-start | bytes 1572868
  3.4 40.2 %collective-permute-start = (bf16[8,19,256]{2,1,0:T(8,128)(2,1)}, bf16[8,19,256]{2,1,0:T(8,128)(2,1)S(1)}, u32[]{:S(2)}, u32[]{:S(2)}) collective-permute-start(bf16[8,19,256]{2,1,0:T(8,128)(2,1)} %get-tuple-element.407), channel_id=1, source_target_pairs={{0,1},{1,2},{2,3},{3,4},{4,5},{5,6},{6,7},{7,8},{8,9},{9,10},{10,1... | collective-permute-start | bytes 233480 | tf_op jit(solution)/shard_map/ppermute | solution.py:20
  7.3 36.3 %collective-permute-start.1 = (bf16[8,19,256]{2,1,0:T(8,128)(2,1)S(1)}, bf16[8,19,256]{2,1,0:T(8,128)(2,1)}, u32[]{:S(2)}, u32[]{:S(2)}) collective-permute-start(bf16[8,19,256]{2,1,0:T(8,128)(2,1)S(1)} %get-tuple-element.408), channel_id=1, source_target_pairs={{1,0},{2,1},{3,2},{4,3},{5,4},{6,5},{7,6},{8,7},{9,8},{10,9},{11,1... | collective-permute-start | bytes 233480 | tf_op jit(solution)/shard_map/ppermute | solution.py:23
  23.7 610.9 %all-to-all-start = ((bf16[128,4,1216]{2,1,0:T(4,128)(2,1)}), bf16[128,4,1216]{2,1,0:T(4,128)(2,1)}, u32[]{:S(2)}, u32[]{:S(2)}) async-start(bf16[128,4,1216]{2,1,0:T(4,128)(2,1)} %reshape.212), calls=%async_computation | async-start | bytes 2621440 | tf_op jit(solution)/shard_map/all_to_all | solution.py:109
  60.4 24.9 %copy-start.8 = (f32[8,12,256]{2,1,0:T(8,128)S(1)}, f32[8,12,256]{2,1,0:T(8,128)}, u32[]{:S(2)}) copy-start(f32[8,12,256]{2,1,0:T(8,128)} %get-tuple-element.549) | copy-start | bytes 294916 | tf_op jit(solution)/shard_map/while
  60.4 24.9 %copy-start.11 = (f32[8,256]{1,0:T(8,128)S(1)}, f32[8,256]{1,0:T(8,128)}, u32[]{:S(2)}) copy-start(f32[8,256]{1,0:T(8,128)} %get-tuple-element.548) | copy-start | bytes 24580 | tf_op jit(solution)/shard_map/while
  60.4 24.9 %copy-start.12 = (f32[8,256]{1,0:T(8,128)S(1)}, f32[8,256]{1,0:T(8,128)}, u32[]{:S(2)}) copy-start(f32[8,256]{1,0:T(8,128)} %get-tuple-element.550) | copy-start | bytes 24580 | tf_op jit(solution)/shard_map/while
  85.3 33.9 %copy-start.5 = (bf16[80,3,256]{2,1,0:T(4,128)(2,1)S(1)}, bf16[80,3,256]{2,1,0:T(4,128)(2,1)}, u32[]{:S(2)}) copy-start(bf16[80,3,256]{2,1,0:T(4,128)(2,1)} %copy-done.4) | copy-start | bytes 368644 | tf_op jit(solution)/shard_map/while
  132.2 24.9 %copy-start.8 = (f32[8,12,256]{2,1,0:T(8,128)S(1)}, f32[8,12,256]{2,1,0:T(8,128)}, u32[]{:S(2)}) copy-start(f32[8,12,256]{2,1,0:T(8,128)} %get-tuple-element.549) | copy-start | bytes 294916 | tf_op jit(solution)/shard_map/while
  132.2 24.9 %copy-start.11 = (f32[8,256]{1,0:T(8,128)S(1)}, f32[8,256]{1,0:T(8,128)}, u32[]{:S(2)}) copy-start(f32[8,256]{1,0:T(8,128)} %get-tuple-element.548) | copy-start | bytes 24580 | tf_op jit(solution)/shard_map/while
  132.2 24.9 %copy-start.12 = (f32[8,256]{1,0:T(8,128)S(1)}, f32[8,256]{1,0:T(8,128)}, u32[]{:S(2)}) copy-start(f32[8,256]{1,0:T(8,128)} %get-tuple-element.550) | copy-start | bytes 24580 | tf_op jit(solution)/shard_map/while
  157.1 33.9 %copy-start.5 = (bf16[80,3,256]{2,1,0:T(4,128)(2,1)S(1)}, bf16[80,3,256]{2,1,0:T(4,128)(2,1)}, u32[]{:S(2)}) copy-start(bf16[80,3,256]{2,1,0:T(4,128)(2,1)} %copy-done.4) | copy-start | bytes 368644 | tf_op jit(solution)/shard_map/while
  203.9 24.9 %copy-start.8 = (f32[8,12,256]{2,1,0:T(8,128)S(1)}, f32[8,12,256]{2,1,0:T(8,128)}, u32[]{:S(2)}) copy-start(f32[8,12,256]{2,1,0:T(8,128)} %get-tuple-element.549) | copy-start | bytes 294916 | tf_op jit(solution)/shard_map/while
  203.9 24.9 %copy-start.11 = (f32[8,256]{1,0:T(8,128)S(1)}, f32[8,256]{1,0:T(8,128)}, u32[]{:S(2)}) copy-start(f32[8,256]{1,0:T(8,128)} %get-tuple-element.548) | copy-start | bytes 24580 | tf_op jit(solution)/shard_map/while
  203.9 24.9 %copy-start.12 = (f32[8,256]{1,0:T(8,128)S(1)}, f32[8,256]{1,0:T(8,128)}, u32[]{:S(2)}) copy-start(f32[8,256]{1,0:T(8,128)} %get-tuple-element.550) | copy-start | bytes 24580 | tf_op jit(solution)/shard_map/while
  228.8 33.9 %copy-start.5 = (bf16[80,3,256]{2,1,0:T(4,128)(2,1)S(1)}, bf16[80,3,256]{2,1,0:T(4,128)(2,1)}, u32[]{:S(2)}) copy-start(bf16[80,3,256]{2,1,0:T(4,128)(2,1)} %copy-done.4) | copy-start | bytes 368644 | tf_op jit(solution)/shard_map/while
  275.7 24.9 %copy-start.8 = (f32[8,12,256]{2,1,0:T(8,128)S(1)}, f32[8,12,256]{2,1,0:T(8,128)}, u32[]{:S(2)}) copy-start(f32[8,12,256]{2,1,0:T(8,128)} %get-tuple-element.549) | copy-start | bytes 294916 | tf_op jit(solution)/shard_map/while
  275.7 24.9 %copy-start.11 = (f32[8,256]{1,0:T(8,128)S(1)}, f32[8,256]{1,0:T(8,128)}, u32[]{:S(2)}) copy-start(f32[8,256]{1,0:T(8,128)} %get-tuple-element.548) | copy-start | bytes 24580 | tf_op jit(solution)/shard_map/while
  275.7 24.9 %copy-start.12 = (f32[8,256]{1,0:T(8,128)S(1)}, f32[8,256]{1,0:T(8,128)}, u32[]{:S(2)}) copy-start(f32[8,256]{1,0:T(8,128)} %get-tuple-element.550) | copy-start | bytes 24580 | tf_op jit(solution)/shard_map/while
  300.6 33.9 %copy-start.5 = (bf16[80,3,256]{2,1,0:T(4,128)(2,1)S(1)}, bf16[80,3,256]{2,1,0:T(4,128)(2,1)}, u32[]{:S(2)}) copy-start(bf16[80,3,256]{2,1,0:T(4,128)(2,1)} %copy-done.4) | copy-start | bytes 368644 | tf_op jit(solution)/shard_map/while
  347.4 24.9 %copy-start.8 = (f32[8,12,256]{2,1,0:T(8,128)S(1)}, f32[8,12,256]{2,1,0:T(8,128)}, u32[]{:S(2)}) copy-start(f32[8,12,256]{2,1,0:T(8,128)} %get-tuple-element.549) | copy-start | bytes 294916 | tf_op jit(solution)/shard_map/while
  347.4 24.9 %copy-start.11 = (f32[8,256]{1,0:T(8,128)S(1)}, f32[8,256]{1,0:T(8,128)}, u32[]{:S(2)}) copy-start(f32[8,256]{1,0:T(8,128)} %get-tuple-element.548) | copy-start | bytes 24580 | tf_op jit(solution)/shard_map/while
  347.4 24.9 %copy-start.12 = (f32[8,256]{1,0:T(8,128)S(1)}, f32[8,256]{1,0:T(8,128)}, u32[]{:S(2)}) copy-start(f32[8,256]{1,0:T(8,128)} %get-tuple-element.550) | copy-start | bytes 24580 | tf_op jit(solution)/shard_map/while
  372.3 33.9 %copy-start.5 = (bf16[80,3,256]{2,1,0:T(4,128)(2,1)S(1)}, bf16[80,3,256]{2,1,0:T(4,128)(2,1)}, u32[]{:S(2)}) copy-start(bf16[80,3,256]{2,1,0:T(4,128)(2,1)} %copy-done.4) | copy-start | bytes 368644 | tf_op jit(solution)/shard_map/while
  419.1 24.9 %copy-start.8 = (f32[8,12,256]{2,1,0:T(8,128)S(1)}, f32[8,12,256]{2,1,0:T(8,128)}, u32[]{:S(2)}) copy-start(f32[8,12,256]{2,1,0:T(8,128)} %get-tuple-element.549) | copy-start | bytes 294916 | tf_op jit(solution)/shard_map/while
  419.1 24.9 %copy-start.11 = (f32[8,256]{1,0:T(8,128)S(1)}, f32[8,256]{1,0:T(8,128)}, u32[]{:S(2)}) copy-start(f32[8,256]{1,0:T(8,128)} %get-tuple-element.548) | copy-start | bytes 24580 | tf_op jit(solution)/shard_map/while
  419.2 24.9 %copy-start.12 = (f32[8,256]{1,0:T(8,128)S(1)}, f32[8,256]{1,0:T(8,128)}, u32[]{:S(2)}) copy-start(f32[8,256]{1,0:T(8,128)} %get-tuple-element.550) | copy-start | bytes 24580 | tf_op jit(solution)/shard_map/while
  444.1 33.9 %copy-start.5 = (bf16[80,3,256]{2,1,0:T(4,128)(2,1)S(1)}, bf16[80,3,256]{2,1,0:T(4,128)(2,1)}, u32[]{:S(2)}) copy-start(bf16[80,3,256]{2,1,0:T(4,128)(2,1)} %copy-done.4) | copy-start | bytes 368644 | tf_op jit(solution)/shard_map/while
  490.9 24.9 %copy-start.8 = (f32[8,12,256]{2,1,0:T(8,128)S(1)}, f32[8,12,256]{2,1,0:T(8,128)}, u32[]{:S(2)}) copy-start(f32[8,12,256]{2,1,0:T(8,128)} %get-tuple-element.549) | copy-start | bytes 294916 | tf_op jit(solution)/shard_map/while
  490.9 24.9 %copy-start.11 = (f32[8,256]{1,0:T(8,128)S(1)}, f32[8,256]{1,0:T(8,128)}, u32[]{:S(2)}) copy-start(f32[8,256]{1,0:T(8,128)} %get-tuple-element.548) | copy-start | bytes 24580 | tf_op jit(solution)/shard_map/while
  490.9 24.9 %copy-start.12 = (f32[8,256]{1,0:T(8,128)S(1)}, f32[8,256]{1,0:T(8,128)}, u32[]{:S(2)}) copy-start(f32[8,256]{1,0:T(8,128)} %get-tuple-element.550) | copy-start | bytes 24580 | tf_op jit(solution)/shard_map/while
  515.8 33.9 %copy-start.5 = (bf16[80,3,256]{2,1,0:T(4,128)(2,1)S(1)}, bf16[80,3,256]{2,1,0:T(4,128)(2,1)}, u32[]{:S(2)}) copy-start(bf16[80,3,256]{2,1,0:T(4,128)(2,1)} %copy-done.4) | copy-start | bytes 368644 | tf_op jit(solution)/shard_map/while
  562.6 24.9 %copy-start.11 = (f32[8,256]{1,0:T(8,128)S(1)}, f32[8,256]{1,0:T(8,128)}, u32[]{:S(2)}) copy-start(f32[8,256]{1,0:T(8,128)} %get-tuple-element.548) | copy-start | bytes 24580 | tf_op jit(solution)/shard_map/while
  562.6 24.9 %copy-start.12 = (f32[8,256]{1,0:T(8,128)S(1)}, f32[8,256]{1,0:T(8,128)}, u32[]{:S(2)}) copy-start(f32[8,256]{1,0:T(8,128)} %get-tuple-element.550) | copy-start | bytes 24580 | tf_op jit(solution)/shard_map/while
  587.5 33.9 %copy-start.5 = (bf16[80,3,256]{2,1,0:T(4,128)(2,1)S(1)}, bf16[80,3,256]{2,1,0:T(4,128)(2,1)}, u32[]{:S(2)}) copy-start(bf16[80,3,256]{2,1,0:T(4,128)(2,1)} %copy-done.4) | copy-start | bytes 368644 | tf_op jit(solution)/shard_map/while
  656.9 31.7 %copy-start.9 = (bf16[2,32,64,16]{2,3,1,0:T(8,128)(2,1)S(1)}, bf16[2,32,64,16]{2,3,1,0:T(8,128)(2,1)}, u32[]{:S(2)}) copy-start(bf16[2,32,64,16]{2,3,1,0:T(8,128)(2,1)} %custom-call.8) | copy-start | bytes 393220
  656.9 31.7 %copy-start.15 = (s32[2]{0:T(128)S(1)}, s32[2]{0:T(128)}, u32[]{:S(2)}) copy-start(s32[2]{0:T(128)} %iota_multiply_fusion) | copy-start | bytes 28
  725.0 60.4 %copy-start.1 = (f32[32,64,64]{2,1,0:T(8,128)S(1)}, f32[32,64,64]{2,1,0:T(8,128)}, u32[]{:S(2)}) copy-start(f32[32,64,64]{2,1,0:T(8,128)} %get-tuple-element.528) | copy-start | bytes 1572868 | tf_op jit(solution)/shard_map/while
  725.0 60.5 %copy-start.2 = (f32[32,64,64]{2,1,0:T(8,128)S(1)}, f32[32,64,64]{2,1,0:T(8,128)}, u32[]{:S(2)}) copy-start(f32[32,64,64]{2,1,0:T(8,128)} %get-tuple-element.530) | copy-start | bytes 1572868 | tf_op jit(solution)/shard_map/while
  725.0 60.5 %copy-start.10 = (bf16[64,64,16]{1,2,0:T(8,128)(2,1)S(1)}, bf16[64,64,16]{1,2,0:T(8,128)(2,1)}, u32[]{:S(2)}) copy-start(bf16[64,64,16]{1,2,0:T(8,128)(2,1)} %get-tuple-element.630) | copy-start | bytes 393220 | tf_op jit(solution)/shard_map/while
  908.8 60.4 %copy-start.1 = (f32[32,64,64]{2,1,0:T(8,128)S(1)}, f32[32,64,64]{2,1,0:T(8,128)}, u32[]{:S(2)}) copy-start(f32[32,64,64]{2,1,0:T(8,128)} %get-tuple-element.528) | copy-start | bytes 1572868 | tf_op jit(solution)/shard_map/while
  908.8 60.5 %copy-start.2 = (f32[32,64,64]{2,1,0:T(8,128)S(1)}, f32[32,64,64]{2,1,0:T(8,128)}, u32[]{:S(2)}) copy-start(f32[32,64,64]{2,1,0:T(8,128)} %get-tuple-element.530) | copy-start | bytes 1572868 | tf_op jit(solution)/shard_map/while
  908.8 60.5 %copy-start.10 = (bf16[64,64,16]{1,2,0:T(8,128)(2,1)S(1)}, bf16[64,64,16]{1,2,0:T(8,128)(2,1)}, u32[]{:S(2)}) copy-start(bf16[64,64,16]{1,2,0:T(8,128)(2,1)} %get-tuple-element.630) | copy-start | bytes 393220 | tf_op jit(solution)/shard_map/while
  1084.3 76.1 %copy-start.14 = (s32[1,128,4]{1,2,0:T(4,128)S(1)}, s32[1,128,4]{1,2,0:T(4,128)}, u32[]{:S(2)}) copy-start(s32[1,128,4]{1,2,0:T(4,128)} %param.25) | copy-start | bytes 6148
  1142.5 30.1 %all-to-all-start.1 = ((bf16[128,4,1024]{2,1,0:T(4,128)(2,1)}), bf16[128,4,1024]{2,1,0:T(4,128)(2,1)}, u32[]{:S(2)}, u32[]{:S(2)}) async-start(bf16[128,4,1024]{2,1,0:T(4,128)(2,1)} %convert_element_type.61), calls=%async_computation.1 | async-start | bytes 2097152 | tf_op jit(solution)/shard_map/all_to_all | solution.py:164
  1153.6 14.6 %collective-permute-start.2 = (bf16[8,16,256]{2,1,0:T(8,128)(2,1)S(1)}, bf16[8,16,256]{2,1,0:T(8,128)(2,1)}, u32[]{:S(2)}, u32[]{:S(2)}) collective-permute-start(bf16[8,16,256]{2,1,0:T(8,128)(2,1)S(1)} %get-tuple-element.405), channel_id=1, source_target_pairs={{0,1},{1,2},{2,3},{3,4},{4,5},{5,6},{6,7},{7,8},{8,9},{9,10},{10,1... | collective-permute-start | bytes 196616 | tf_op jit(solution)/shard_map/ppermute | solution.py:20
  1156.9 11.3 collective-permute-start.3
  (35 other events, 532.1 us)
where the time goes:
time: 1190 us; the launch traced here: 1180 us
  matrix products  639 us (54%)
  local copies, waits for them, and re-layouts  309 us (26%)
  other arithmetic  152 us (13%)
  loops' own time  41.9 us (4%)
  starting transfers between devices  34.7 us (3%)
    dot_general x8, matrix products, group_step(): jnp.einsum('gmab,gmrb->gra', kernel, target_probe, preferred_element_type...  199 us
    dot_general x8, matrix products, group_step(): jnp.einsum('gmab,gra->gmrb', kernel, own_w, preferred_element_type=jnp.fl...  193 us
    dot_general x2, matrix products, far_step(): jnp.einsum('gmkl,gmlr->gkr', coupling, coef_far, preferred_element_type=j...  121 us
    dot_general x2, matrix products, far_step(): jnp.einsum('gmkl,gkr->gmlr', coupling, back_own, preferred_element_type=j...  113 us
    scatter-add x8, other arithmetic, group_step(): window.at[local_pos.reshape(-1)]  71.3 us
    dynamic_update_slice x4, local copies, waits for them, and re-layouts, local(): far_in, returned = lax.map(far_step, far_begins)  61.4 us
    dynamic_slice x4, local copies, waits for them, and re-layouts, far_step(): coef_far = lax.dynamic_slice_in_dim(remote_coef, begin_row, far_rows, 0)  48.7 us
    reshape x2, local copies, waits for them, and re-layouts, local(): returned.reshape(leaf_count * far_count, coef_width)  45.4 us
  transfers between devices with their start and end apart: 6, of which 1 were waited for; matrix products, arithmetic and copies ran while one was open for 49% of the time, Pallas kernels for 0%

commit v1 on v0

v1 whole, which is shorter than its diff:
```python
import functools

import jax
import jax.numpy as jnp
from jax import lax
from jax.experimental import pallas as pl
from jax.experimental.pallas import tpu as pltpu
from jax.sharding import PartitionSpec as P

REACH = 8
SCALE = 3.0**0.5 / 0.5
LOG2E = 1.4426950408889634
SOFTENING = 0.01
NUGGET = 0.5
LEAVES = 64
EXT = LEAVES + 2 * REACH
BAND = REACH + 1
RHS = 16
SIZE = 256
RANK = 64
CAP = 4
PEERS = 128
SLOTS = PEERS * CAP
FAR = 64
bf16 = jnp.bfloat16
f32 = jnp.float32
VMEM = pl.BlockSpec(memory_space=pltpu.VMEM)
SMEM = pl.BlockSpec(memory_space=pltpu.SMEM)


def params(mib=60):
    return pltpu.CompilerParams(vmem_limit_bytes=mib * 2**20)


def kappa(v):
    s = v * lax.rsqrt(v)
    return ((s * (0.5 * SCALE) + 0.5) * jnp.exp2(s * (-SCALE * LOG2E))).astype(bf16)


def split3(n):
    a = n.astype(bf16).astype(f32)
    b = (n - a).astype(bf16).astype(f32)
    return a, b, n - a - b


def stack_rows(rows, height, width):
    at = lax.broadcasted_iota(jnp.int32, (height, width), 0)
    out = jnp.zeros((height, width), f32)
    for r, value in enumerate(rows):
        out = jnp.where(at == r, value, out)
    return out


def point_features(xyz):
    x, y, z = xyz
    n = x * x + y * y + z * z
    one = jnp.ones_like(x)
    right = [x, y, z, *split3(n), one, one, one]
    left = [-2.0 * x, -2.0 * y, -2.0 * z, one, one, one, *split3(n + SOFTENING)]
    return left, right


def prep_kernel(probe, weights, sk, row_basis, col_basis, send, out, back, own, coef_t, feat_t):
    low = lax.broadcasted_iota(jnp.int32, (RHS, 128), 1) < RANK
    low8 = lax.broadcasted_iota(jnp.int32, (8, 128), 1) < RANK

    def leaf(j, _):
        nt = (((1,), (1,)), ((), ()))
        c = lax.dot_general(probe[j], col_basis[j], nt, preferred_element_type=f32)
        coef_t[j] = jnp.concatenate([c, c], axis=1).astype(bf16)
        b = lax.dot_general(weights[j], row_basis[j], nt, preferred_element_type=f32)
        back[j] = b.astype(bf16)
        rows = sk[j].astype(f32)
        left, right = point_features((rows[0:1], rows[1:2], rows[2:3]))
        feat_t[j] = stack_rows(right[:8], 8, 128)
        own[j] = stack_rows(left, 128, 128)[:, :RANK].T.astype(bf16)
        return 0

    lax.fori_loop(0, LEAVES, leaf, 0)

    def peer(d, _):
        at = [send[d * CAP + q] for q in range(CAP)]
        for h in range(2):
            out[d, :, h * 128 : (h + 1) * 128] = jnp.where(low, coef_t[at[2 * h]], coef_t[at[2 * h + 1]])
        f = [jnp.where(low8, feat_t[at[2 * h]], feat_t[at[2 * h + 1]]) for h in range(2)]
        out[d, :, 256:384] = jnp.concatenate(f, axis=0).astype(bf16)
        return 0

    lax.fori_loop(0, PEERS, peer, 0)


def prep(probe, weights, sk, row_basis, col_basis, send):
    return pl.pallas_call(
        prep_kernel,
        out_shape=(
            jax.ShapeDtypeStruct((PEERS, RHS, 384), bf16),
            jax.ShapeDtypeStruct((LEAVES, RHS, RANK), bf16),
            jax.ShapeDtypeStruct((LEAVES, RANK, 128), bf16),
        ),
        in_specs=[VMEM] * 5 + [SMEM],
        out_specs=(VMEM,) * 3,
        scratch_shapes=[pltpu.VMEM((LEAVES, RHS, 128), bf16), pltpu.VMEM((LEAVES, 8, 128), f32)],
        compiler_params=params(),
        name="prep",
    )(probe, weights, sk, row_basis, col_basis, send)


def near_kernel(ext, cf, cb, out, ks, va, acc, left_t, right_t):
    acc[...] = jnp.zeros_like(acc)

    def features(j):
        rows = ext[j, 32:48, :].astype(f32)
        left, right = point_features((rows[0:1], rows[1:2], rows[2:3]))
        right_t[j] = stack_rows(right, 16, SIZE).astype(bf16)
        left_t[j] = stack_rows(left, 128, SIZE).T.astype(bf16)

    def first(j, _):
        features(j)
        return 0

    lax.fori_loop(0, BAND, first, 0)

    def body(j, _):
        right = right_t[j]
        vj = ext[j, 0:32, :]
        for b in range(BAND):
            i = j - REACH + b
            v = jnp.dot(left_t[i, :, 0:16], right, preferred_element_type=f32)
            ks[b * SIZE : (b + 1) * SIZE, :] = kappa(v)
        for b in range(BAND):
            i = j - REACH + b
            d = REACH - b
            c1 = cf[i * BAND + d].astype(bf16)
            c2 = cb[i * BAND + d].astype(bf16)
            vi = ext[i, 0:32, :]
            va[0:16, b * SIZE : (b + 1) * SIZE] = vi[0:16] * c2
            va[16:32, b * SIZE : (b + 1) * SIZE] = vi[16:32] * c1
            if b < REACH:
                vb = jnp.concatenate([vj[0:16] * c1, vj[16:32] * c2], axis=0)
                acc[i] += lax.dot_general(
                    vb, ks[b * SIZE : (b + 1) * SIZE, :], (((1,), (1,)), ((), ())), preferred_element_type=f32
                )
        acc[j] += jnp.dot(va[...], ks[...], preferred_element_type=f32) + (NUGGET * cf[j * BAND]) * vj.astype(f32)
        features(jnp.minimum(j + 1, EXT - 1))
        return 0

    lax.fori_loop(REACH, EXT, body, 0)
    out[...] = acc[REACH : REACH + LEAVES]


def near(ext, cf, cb):
    return pl.pallas_call(
        near_kernel,
        out_shape=jax.ShapeDtypeStruct((LEAVES, 2 * RHS, SIZE), f32),
        in_specs=[VMEM, SMEM, SMEM],
        out_specs=VMEM,
        scratch_shapes=[
            pltpu.VMEM((BAND * SIZE, SIZE), bf16),
            pltpu.VMEM((2 * RHS, BAND * SIZE), bf16),
            pltpu.VMEM((EXT, 2 * RHS, SIZE), f32),
            pltpu.VMEM((EXT, SIZE, 128), bf16),
            pltpu.VMEM((EXT, 16, SIZE), bf16),
        ],
        compiler_params=params(),
        name="near",
    )(ext, cf, cb)


def far_kernel(arrived, own, back, slot, far_in, ret, feat, coef, gt, ct, ks, rt, acc_l, acc_u):
    low = lax.broadcasted_iota(jnp.int32, (RHS, 128), 1) < RANK
    low8 = lax.broadcasted_iota(jnp.int32, (8, 128), 1) < RANK
    tail = jnp.where(lax.broadcasted_iota(jnp.int32, (8, 128), 0) == 0, 1.0, 0.0).astype(f32)

    def both(x, mask):
        y = pltpu.roll(x, RANK, 1)
        return jnp.where(mask, x, y), jnp.where(mask, y, x)

    def table(d, _):
        for h in range(2):
            c = both(arrived[d, :, h * 128 : (h + 1) * 128].astype(f32), low)
            f = both(arrived[d, :, 256:384].astype(f32)[h * 8 : (h + 1) * 8], low8)
            for q in range(2):
                coef[d * CAP + 2 * h + q] = c[q].astype(bf16)
                feat[d * CAP + 2 * h + q] = jnp.concatenate([f[q], tail], axis=0).astype(bf16)
        return 0

    lax.fori_loop(0, PEERS, table, 0)
    acc_l[...] = jnp.zeros_like(acc_l)
    acc_u[...] = jnp.zeros_like(acc_u)

    def leaf(i, _):
        at = [slot[i * FAR + m] for m in range(FAR)]
        for p in range(FAR // 2):
            lanes = slice(p * 128, (p + 1) * 128)
            gt[:, lanes] = jnp.where(low, feat[at[2 * p]], feat[at[2 * p + 1]])
            ct[:, lanes] = jnp.where(low, coef[at[2 * p]], coef[at[2 * p + 1]])
        mine = own[i, :, 0:16]
        for t in range(16):
            lanes = slice(t * 256, (t + 1) * 256)
            ks[:, lanes] = kappa(jnp.dot(mine, gt[:, lanes], preferred_element_type=f32))
        far_in[i] = lax.dot_general(
            ct[...], ks[...], (((1,), (1,)), ((), ())), preferred_element_type=f32
        ).astype(bf16)
        rt[...] = jnp.dot(back[i], ks[...], preferred_element_type=f32)
        for p in range(FAR // 2):
            tile = rt[:, p * 128 : (p + 1) * 128]
            acc_l[at[2 * p]] += tile
            acc_u[at[2 * p + 1]] += tile
        return 0

    lax.fori_loop(0, LEAVES, leaf, 0)

    def pack(d, _):
        for h in range(2):
            s = d * CAP + 2 * h
            even = acc_l[s] + pltpu.roll(acc_u[s], RANK, 1)
            odd = pltpu.roll(acc_l[s + 1], RANK, 1) + acc_u[s + 1]
            ret[d, :, h * 128 : (h + 1) * 128] = jnp.where(low, even, odd).astype(bf16)
        return 0

    lax.fori_loop(0, PEERS, pack, 0)


def far(arrived, own, back, slot):
    return pl.pallas_call(
        far_kernel,
        out_shape=(
            jax.ShapeDtypeStruct((LEAVES, RHS, RANK), bf16),
            jax.ShapeDtypeStruct((PEERS, RHS, 256), bf16),
        ),
        in_specs=[VMEM] * 3 + [SMEM],
        out_specs=(VMEM,) * 2,
        scratch_shapes=[
            pltpu.VMEM((SLOTS, 16, 128), bf16),
            pltpu.VMEM((SLOTS, RHS, 128), bf16),
            pltpu.VMEM((16, FAR * RANK), bf16),
            pltpu.VMEM((RHS, FAR * RANK), bf16),
            pltpu.VMEM((RANK, FAR * RANK), bf16),
            pltpu.VMEM((RHS, FAR * RANK), f32),
            pltpu.VMEM((SLOTS, RHS, 128), f32),
            pltpu.VMEM((SLOTS, RHS, 128), f32),
        ],
        compiler_params=params(),
        name="far",
    )(arrived, own, back, slot)


def post_kernel(came, send, near_out, far_in, row_basis, col_basis, product, adjoint, acc_l, acc_u):
    acc_l[...] = jnp.zeros_like(acc_l)
    acc_u[...] = jnp.zeros_like(acc_u)

    def peer(d, _):
        for h in range(2):
            tile = came[d, :, h * 128 : (h + 1) * 128].astype(f32)
            acc_l[send[d * CAP + 2 * h]] += tile
            acc_u[send[d * CAP + 2 * h + 1]] += tile
        return 0

    lax.fori_loop(0, PEERS, peer, 0)

    def leaf(j, _):
        total = (acc_l[j] + pltpu.roll(acc_u[j], RANK, 1))[:, :RANK].astype(bf16)
        adjoint[j] = near_out[j, RHS:, :] + jnp.dot(total, col_basis[j], preferred_element_type=f32)
        product[j] = near_out[j, :RHS, :] + jnp.dot(far_in[j], row_basis[j], preferred_element_type=f32)
        return 0

    lax.fori_loop(0, LEAVES, leaf, 0)


def post(came, send, near_out, far_in, row_basis, col_basis):
    return pl.pallas_call(
        post_kernel,
        out_shape=(jax.ShapeDtypeStruct((LEAVES, RHS, SIZE), f32),) * 2,
        in_specs=[VMEM, SMEM] + [VMEM] * 4,
        out_specs=(VMEM,) * 2,
        scratch_shapes=[pltpu.VMEM((LEAVES, RHS, 128), f32)] * 2,
        compiler_params=params(),
        name="post",
    )(came, send, near_out, far_in, row_basis, col_basis)


def local(probe, weights, points, skeleton, row_basis, col_basis, near_leaf, far_slot, send_leaf):
    axes = ("leaf", "sub")
    count = lax.axis_size(axes)
    first_leaf = lax.axis_index(axes) * LEAVES
    own_id = first_leaf + jnp.arange(LEAVES, dtype=jnp.int32)
    offsets = jnp.arange(-REACH, REACH + 1, dtype=jnp.int32)
    hits = (near_leaf[:, :, None] - own_id[:, None, None]) == offsets
    counts = jnp.sum(hits.astype(f32), axis=1).astype(bf16)
    counts = jnp.pad(counts, ((0, 0), (0, SIZE - 2 * REACH - 1)))
    block = jnp.concatenate(
        [probe, weights, points, counts[:, None, :], jnp.zeros((LEAVES, 12, SIZE), bf16)], axis=1
    )
    ahead = [(i, i + 1) for i in range(count - 1)]
    behind = [(b, a) for a, b in ahead]
    below = lax.ppermute(block[LEAVES - REACH :], axes, ahead)
    above = lax.ppermute(block[:REACH], axes, behind)
    ext = jnp.concatenate([below, block, above], axis=0)
    cnt = ext[:, 35, : 2 * REACH + 1].astype(f32)
    cf = cnt[: EXT, REACH:]
    cnt_more = jnp.pad(cnt, ((0, REACH), (0, 0)))
    cb = jnp.stack([cnt_more[d : d + EXT, REACH - d] for d in range(BAND)], axis=1)
    send = send_leaf.reshape(SLOTS)
    sk = skeleton.reshape(LEAVES, 3, RANK)
    sk = jnp.concatenate([sk, sk], axis=2)
    payload, back, own = prep(probe, weights, sk, row_basis, col_basis, send)
    arrived = lax.all_to_all(payload, axes, split_axis=0, concat_axis=0, tiled=True)
    near_out = near(ext, cf.reshape(-1), cb.reshape(-1))
    far_in, ret = far(arrived, own, back, far_slot.reshape(-1))
    came = lax.all_to_all(ret, axes, split_axis=0, concat_axis=0, tiled=True)
    return post(came, send, near_out, far_in, row_basis, col_basis)


def solution(mesh):
    lead = P(("leaf", "sub"), None, None)
    flat = P(("leaf", "sub"), None)
    return jax.shard_map(
        local,
        mesh=mesh,
        in_specs=(lead, lead, lead, flat, lead, lead, flat, flat, lead),
        out_specs=(lead, lead),
        check_vma=False,
    )
```

time: 1190 us -> 260 us (0.22)
  matrix products: 639 us -> 0 us
  local copies, waits for them, and re-layouts: 309 us -> 17.4 us
  Pallas kernels: 0 us -> 191 us
  other arithmetic: 152 us -> 1.16 us
  loops' own time: 41.9 us -> 0 us
  waiting for transfers between devices: 6.28 us -> 25.1 us
  starting transfers between devices: 34.7 us -> 22.8 us
    dot_general x25 -> x0, matrix products: 639 us -> none  [the longest x8 199 us: group_step(): jnp.einsum('gmab,gmrb->gra', kernel, target_probe, preferred_element_type...]
    pallas_call x0 -> x4, Pallas kernels: none -> 191 us  [the longest x1 88.8 us: near(): pl.pallas_call(near_kernel, out_shape=jax.ShapeDtypeStruct((LEAVES, 2 * R...]
    scatter-add x11 -> x0, other arithmetic: 111 us -> none  [the longest x8 71.3 us: group_step(): window.at[local_pos.reshape(-1)]]
    dynamic_slice x34 -> x0, local copies, waits for them, and re-layouts: 84.6 us -> none  [the longest x4 48.7 us: far_step(): coef_far = lax.dynamic_slice_in_dim(remote_coef, begin_row, far_rows, 0)]
    dynamic_update_slice x12 -> x0, local copies, waits for them, and re-layouts: 67.7 us -> none  [the longest x4 61.4 us: local(): far_in, returned = lax.map(far_step, far_begins)]
    reshape x14 -> x5, local copies, waits for them, and re-layouts: 52.1 us -> 3.21 us  [the longest x2 1.73 us: local(): near_out = near(ext, cf.reshape(-1), cb.reshape(-1))]
    gather x19 -> x0, local copies, waits for them, and re-layouts: 44.5 us -> none  [the longest x1 19.8 us: local(): remote = arrived[far_slot]]
    another operation x2 -> x0, loops' own time: 41.9 us -> none  [the longest x1 37.9 us: near_pass(): padded_acc, forward = lax.scan(group_step, initial, begins)]
  transfers between devices with their start and end apart: 6 -> 4, of which waited for: 1 -> 3; matrix products, arithmetic and copies ran while one was open for 49% -> 5% of each run, Pallas kernels for 0% -> 34%
where the time goes in v1:
time: 260 us; the launch traced here: 258 us
  Pallas kernels  191 us (73%)
  waiting for transfers between devices  25.1 us (10%)
  starting transfers between devices  22.8 us (9%)
  local copies, waits for them, and re-layouts  17.4 us (7%)
    pallas_call x1, Pallas kernels, near(): pl.pallas_call(near_kernel, out_shape=jax.ShapeDtypeStruct((LEAVES, 2 * R...  88.8 us
    pallas_call x1, Pallas kernels, far(): pl.pallas_call(far_kernel, out_shape=(jax.ShapeDtypeStruct((LEAVES, RHS,...  62.7 us
    pallas_call x1, Pallas kernels, prep(): pl.pallas_call(prep_kernel, out_shape=(jax.ShapeDtypeStruct((PEERS, RHS,...  20.6 us
    pallas_call x1, Pallas kernels, post(): pl.pallas_call(post_kernel, out_shape=(jax.ShapeDtypeStruct((LEAVES, RHS,...  18.4 us
    all_to_all x1, waiting for transfers between devices, local(): lax.all_to_all(payload, axes, split_axis=0, concat_axis=0, tiled=True)  13.5 us
    all_to_all x1, starting transfers between devices, local(): lax.all_to_all(payload, axes, split_axis=0, concat_axis=0, tiled=True)  11.5 us
    concatenate x1, local copies, waits for them, and re-layouts, local(): jnp.concatenate([probe, weights, points, counts[:, None, :], jnp.zeros((L...  9.9 us
    ppermute x1, waiting for transfers between devices, local(): above = lax.ppermute(block[:REACH], axes, behind)  9.83 us
  transfers between devices with their start and end apart: 4, of which 3 were waited for; matrix products, arithmetic and copies ran while one was open for 5% of the time, Pallas kernels for 34%

profile of v1, /device:TPU:1, one launch (start us, length us, event | category | flops | bytes accessed | tf_op | source)
XLA Modules:
  0.0 257.8 jit_solution(4422300585782649552)
XLA Ops:
  0.6 0.9 copy.37
  1.5 0.1 copy.38
  1.6 0.7 pad_maximum_fusion.1.sk
  2.4 0.8 copy.40
  3.2 0.7 reshape.34.send
  3.8 20.6 %prep.1 = (bf16[128,16,384]{2,1,0:T(8,128)(2,1)}, bf16[64,16,64]{2,1,0:T(8,128)(2,1)}, bf16[64,64,128]{2,1,0:T(8,128)(2,1)}) custom-call(bf16[64,16,256]{2,1,0:T(8,128)(2,1)} %probe.1, bf16[64,16,256]{2,1,0:T(8,128)(2,1)} %weights.1, bf16[64,3,128]{2,1,0:T(4,128)(2,1)} %pad_maximum_fusion.1.sk, bf16[64,64,256]{2,1,0:T(8,128)(2,1)} %row_basis.3, ...), custom_call_target="tpu_custom_call" | custom-call | tf_op jit(solution)/shard_map/prep/pallas_call | solution.py:93
  24.5 0.0 copy-start.3
  24.5 0.0 copy-start.2
  24.5 0.0 copy-start.4
  24.5 11.5 %all-to-all-start = ((bf16[128,16,384]{2,1,0:T(8,128)(2,1)}), bf16[128,16,384]{2,1,0:T(8,128)(2,1)S(1)}, u32[]{:S(2)}, u32[]{:S(2)}) async-start(bf16[128,16,384]{2,1,0:T(8,128)(2,1)} %get-tuple-element.7), calls=%async_computation | async-start | bytes 3145728 | tf_op jit(solution)/shard_map/all_to_all | solution.py:307
  36.0 0.0 copy-done.3
  36.0 0.7 reshape.35.slot
  36.7 0.0 copy-done.2
  36.7 0.1 copy.42
  36.8 0.0 copy-done.4
  36.8 0.1 convert_reduce_fusion
  37.0 0.1 copy.43
  37.1 0.8 broadcast_in_dim.10
  37.9 9.9 %concatenate.10 = bf16[64,48,256]{2,1,0:T(8,128)(2,1)S(1)} concatenate(bf16[64,16,256]{2,1,0:T(8,128)(2,1)} %probe.1, bf16[64,16,256]{2,1,0:T(8,128)(2,1)} %weights.1, bf16[64,3,256]{2,1,0:T(4,128)(2,1)S(1)} %copy.42, bf16[64,1,256]{2,1,0:T(2,128)(2,1)S(1)} %copy.43, bf16[64,12,256]{2,1,0:T(8,128)(2,1)} %broadcast_in_dim.10), dimensions={1} | concatenate | bytes 3145728 | tf_op jit(solution)/shard_map/concatenate | solution.py:291
  47.8 13.5 %all-to-all-done.arrived = bf16[128,16,384]{2,1,0:T(8,128)(2,1)S(1)} async-done(((bf16[128,16,384]{2,1,0:T(8,128)(2,1)}), bf16[128,16,384]{2,1,0:T(8,128)(2,1)S(1)}, u32[]{:S(2)}, u32[]{:S(2)}) %all-to-all-start) | async-done | bytes 1572896 | tf_op jit(solution)/shard_map/all_to_all | solution.py:307
  61.4 0.0 copy-start.1
  61.4 1.2 copy-done.1
  62.5 62.7 %far.1 = (bf16[64,16,64]{2,1,0:T(8,128)(2,1)}, bf16[128,16,256]{2,1,0:T(8,128)(2,1)}) custom-call(bf16[128,16,384]{2,1,0:T(8,128)(2,1)} %copy-done.1, bf16[64,64,128]{2,1,0:T(8,128)(2,1)} %get-tuple-element.8.own, bf16[64,16,64]{2,1,0:T(8,128)(2,1)} %get-tuple-element.9.back, s32[4096]{0:T(1024)} %reshape.35.slot), custom_call_target="tpu_custom_call" | custom-call | tf_op jit(solution)/shard_map/far/pallas_call | solution.py:225
  125.3 4.7 %all-to-all-start.1 = ((bf16[128,16,256]{2,1,0:T(8,128)(2,1)}), bf16[128,16,256]{2,1,0:T(8,128)(2,1)}, u32[]{:S(2)}, u32[]{:S(2)}) async-start(bf16[128,16,256]{2,1,0:T(8,128)(2,1)} %get-tuple-element.10), calls=%async_computation.1 | async-start | bytes 2097152 | tf_op jit(solution)/shard_map/all_to_all | solution.py:310
  130.0 4.7 %collective-permute-start.1 = (bf16[8,48,256]{2,1,0:T(8,128)(2,1)S(1)}, bf16[8,48,256]{2,1,0:T(8,128)(2,1)S(1)}, u32[]{:S(2)}, u32[]{:S(2)}) collective-permute-start(bf16[8,48,256]{2,1,0:T(8,128)(2,1)S(1)} %get-tuple-element.13), channel_id=1, source_target_pairs={{1,0},{2,1},{3,2},{4,3},{5,4},{6,5},{7,6},{8,7},{9,8},{10,9},{11,1... | collective-permute-start | bytes 589832 | tf_op jit(solution)/shard_map/ppermute | solution.py:297
  134.7 1.9 collective-permute-start
  136.6 9.8 %collective-permute-done.1 = bf16[8,48,256]{2,1,0:T(8,128)(2,1)S(1)} collective-permute-done((bf16[8,48,256]{2,1,0:T(8,128)(2,1)S(1)}, bf16[8,48,256]{2,1,0:T(8,128)(2,1)S(1)}, u32[]{:S(2)}, u32[]{:S(2)}) %collective-permute-start.1) | collective-permute-done | bytes 196640 | tf_op jit(solution)/shard_map/ppermute | solution.py:297
  146.5 1.7 collective-permute-done
  148.2 0.2 pad_maximum_fusion.ext
  148.4 0.0 copy-start
  148.5 0.1 slice.56
  148.6 1.0 reshape.36.cf
  149.6 0.1 pad_slice_fusion
  149.7 0.2 stack.3
  149.9 0.7 reshape.37.cb
  150.6 0.0 copy-done
  150.6 88.8 %near.1.near_out = f32[64,32,256]{2,1,0:T(8,128)} custom-call(bf16[80,48,256]{2,1,0:T(8,128)(2,1)} %copy-done, f32[720]{0:T(1024)} %reshape.36.cf, f32[720]{0:T(1024)} %reshape.37.cb), custom_call_target="tpu_custom_call" | custom-call | tf_op jit(solution)/shard_map/near/pallas_call | solution.py:152
  239.4 0.0 all-to-all-done.1.came
  239.5 18.4 %post.1 = (f32[64,16,256]{2,1,0:T(8,128)}, f32[64,16,256]{2,1,0:T(8,128)}) custom-call(bf16[128,16,256]{2,1,0:T(8,128)(2,1)} %all-to-all-done.1.came, s32[512]{0:T(512)} %reshape.34.send, f32[64,32,256]{2,1,0:T(8,128)} %near.1.near_out, bf16[64,16,64]{2,1,0:T(8,128)(2,1)} %get-tuple-element.11.far_in, bf16[64,64,256]{2,1,0:T(8,128)(2,1)} %row_basis.3, ...), custom_call_target="tpu_custom_call" | custom-call | tf_op jit(solution)/shard_map/post/pallas_call | solution.py:271
  (6 shorter events, 0.1 us)
Async XLA Ops:
  24.5 11.5 %copy-start.3 = (s32[64,64]{1,0:T(8,128)S(1)}, s32[64,64]{1,0:T(8,128)}, u32[]{:S(2)}) copy-start(s32[64,64]{1,0:T(8,128)} %param.16) | copy-start | bytes 49156
  24.5 12.2 %copy-start.2 = (bf16[64,3,256]{2,0,1:T(8,128)(2,1)S(1)}, bf16[64,3,256]{2,0,1:T(8,128)(2,1)}, u32[]{:S(2)}) copy-start(bf16[64,3,256]{2,0,1:T(8,128)(2,1)} %param.11) | copy-start | bytes 294916
  24.5 12.3 %copy-start.4 = (s32[64,12]{0,1:T(8,128)S(1)}, s32[64,12]{0,1:T(8,128)}, u32[]{:S(2)}) copy-start(s32[64,12]{0,1:T(8,128)} %param.15) | copy-start | bytes 9220
  24.5 36.9 %all-to-all-start = ((bf16[128,16,384]{2,1,0:T(8,128)(2,1)}), bf16[128,16,384]{2,1,0:T(8,128)(2,1)S(1)}, u32[]{:S(2)}, u32[]{:S(2)}) async-start(bf16[128,16,384]{2,1,0:T(8,128)(2,1)} %get-tuple-element.7), calls=%async_computation | async-start | bytes 3145728 | tf_op jit(solution)/shard_map/all_to_all | solution.py:307
  61.4 1.2 copy-start.1
  125.3 114.2 %all-to-all-start.1 = ((bf16[128,16,256]{2,1,0:T(8,128)(2,1)}), bf16[128,16,256]{2,1,0:T(8,128)(2,1)}, u32[]{:S(2)}, u32[]{:S(2)}) async-start(bf16[128,16,256]{2,1,0:T(8,128)(2,1)} %get-tuple-element.10), calls=%async_computation.1 | async-start | bytes 2097152 | tf_op jit(solution)/shard_map/all_to_all | solution.py:310
  130.0 16.5 %collective-permute-start.1 = (bf16[8,48,256]{2,1,0:T(8,128)(2,1)S(1)}, bf16[8,48,256]{2,1,0:T(8,128)(2,1)S(1)}, u32[]{:S(2)}, u32[]{:S(2)}) collective-permute-start(bf16[8,48,256]{2,1,0:T(8,128)(2,1)S(1)} %get-tuple-element.13), channel_id=1, source_target_pairs={{1,0},{2,1},{3,2},{4,3},{5,4},{6,5},{7,6},{8,7},{9,8},{10,9},{11,1... | collective-permute-start | bytes 589832 | tf_op jit(solution)/shard_map/ppermute | solution.py:297
  134.7 13.5 %collective-permute-start = (bf16[8,48,256]{2,1,0:T(8,128)(2,1)S(1)}, bf16[8,48,256]{2,1,0:T(8,128)(2,1)S(1)}, u32[]{:S(2)}, u32[]{:S(2)}) collective-permute-start(bf16[8,48,256]{2,1,0:T(8,128)(2,1)S(1)} %get-tuple-element.12), channel_id=1, source_target_pairs={{0,1},{1,2},{2,3},{3,4},{4,5},{5,6},{6,7},{7,8},{8,9},{9,10},{10,1... | collective-permute-start | bytes 589832 | tf_op jit(solution)/shard_map/ppermute | solution.py:296
  148.4 2.2 copy-start

commit v2 on v1

v2 whole, which is shorter than its diff:
```python
import functools

import jax
import jax.numpy as jnp
from jax import lax
from jax.experimental import pallas as pl
from jax.experimental.pallas import tpu as pltpu
from jax.sharding import PartitionSpec as P

REACH = 8
SCALE = 3.0**0.5 / 0.5
LOG2E = 1.4426950408889634
SOFTENING = 0.01
NUGGET = 0.5
LEAVES = 64
EXT = LEAVES + 2 * REACH
BAND = REACH + 1
RHS = 16
SIZE = 256
RANK = 64
CAP = 4
PEERS = 128
SLOTS = PEERS * CAP
FAR = 64
bf16 = jnp.bfloat16
f32 = jnp.float32
NT = (((1,), (1,)), ((), ()))
MESH = pl.DeviceIdType.MESH
ROWS = 48
FIRST_COLUMNS = 28
VMEM = pl.BlockSpec(memory_space=pltpu.VMEM)
ANY = pl.BlockSpec(memory_space=pl.ANY)
SMEM = pl.BlockSpec(memory_space=pltpu.SMEM)


def params(mib=60, **more):
    return pltpu.CompilerParams(vmem_limit_bytes=mib * 2**20, **more)


def device_id():
    return lax.axis_index("leaf") * 4 + lax.axis_index("sub")


def kappa(v):
    s = v * lax.rsqrt(v)
    return ((s * (0.5 * SCALE) + 0.5) * jnp.exp2(s * (-SCALE * LOG2E))).astype(bf16)


def split3(n):
    a = n.astype(bf16).astype(f32)
    b = (n - a).astype(bf16).astype(f32)
    return a, b, n - a - b


def stack_rows(rows, height, width):
    at = lax.broadcasted_iota(jnp.int32, (height, width), 0)
    out = jnp.zeros((height, width), f32)
    for r, value in enumerate(rows):
        out = jnp.where(at == r, value, out)
    return out


def point_features(xyz):
    x, y, z = xyz
    n = x * x + y * y + z * z
    one = jnp.ones_like(x)
    right = [x, y, z, *split3(n), one, one, one]
    left = [-2.0 * x, -2.0 * y, -2.0 * z, one, one, one, *split3(n + SOFTENING)]
    return left, right


def prep_kernel(
    probe, weights, points, skeleton, row_basis, col_basis, near_leaf, send, out, back, own, block, coef_t, feat_t, sk, cnt
):
    low = lax.broadcasted_iota(jnp.int32, (RHS, 128), 1) < RANK
    low8 = lax.broadcasted_iota(jnp.int32, (8, 128), 1) < RANK
    low64 = lax.broadcasted_iota(jnp.int32, (LEAVES, 128), 1) < RANK
    xy = skeleton[:, 0:128].astype(f32)
    yx = pltpu.roll(xy, RANK, 1)
    sk[0] = jnp.where(low64, xy, yx)
    sk[1] = jnp.where(low64, yx, xy)
    z = skeleton[:, 128:192].astype(f32)
    sk[2] = jnp.concatenate([z, z], axis=1)
    ids = device_id() * LEAVES + lax.broadcasted_iota(jnp.int32, (LEAVES, 128), 0)
    target = ids + lax.broadcasted_iota(jnp.int32, (LEAVES, 128), 1) - REACH
    total = jnp.zeros((LEAVES, 128), f32)
    for m in range(near_leaf.shape[1]):
        total = total + jnp.where(near_leaf[:, m : m + 1] == target, 1.0, 0.0)
    cnt[...] = jnp.where(lax.broadcasted_iota(jnp.int32, (LEAVES, 128), 1) <= 2 * REACH, total, 0.0)

    def leaf(j, _):
        c = lax.dot_general(probe[j], col_basis[j], NT, preferred_element_type=f32)
        coef_t[j] = jnp.concatenate([c, c], axis=1).astype(bf16)
        back[j] = lax.dot_general(weights[j], row_basis[j], NT, preferred_element_type=f32).astype(bf16)
        left, right = point_features(tuple(sk[k, pl.ds(j, 1), :] for k in range(3)))
        feat_t[j] = stack_rows(right[:8], 8, 128)
        own[j] = stack_rows(left, 128, 128)[:, :RANK].T.astype(bf16)
        block[j, 0:16, :] = probe[j]
        block[j, 16:32, :] = weights[j]
        p = points[j].astype(f32)
        n = cnt[pl.ds(j, 1), :]
        rows = [p[0:1], p[1:2], p[2:3], jnp.concatenate([n, jnp.zeros((1, 128), f32)], axis=1)]
        block[j, 32:48, :] = stack_rows(rows, 16, SIZE).astype(bf16)
        return 0

    lax.fori_loop(0, LEAVES, leaf, 0, unroll=4)

    def peer(d, _):
        at = [send[0, d, q] for q in range(CAP)]
        for h in range(2):
            out[d, :, h * 128 : (h + 1) * 128] = jnp.where(low, coef_t[at[2 * h]], coef_t[at[2 * h + 1]])
        f = [jnp.where(low8, feat_t[at[2 * h]], feat_t[at[2 * h + 1]]) for h in range(2)]
        out[d, :, 256:384] = jnp.concatenate(f, axis=0).astype(bf16)
        return 0

    lax.fori_loop(0, PEERS, peer, 0, unroll=4)


def prep(*operands):
    return pl.pallas_call(
        prep_kernel,
        out_shape=(
            jax.ShapeDtypeStruct((PEERS, RHS, 384), bf16),
            jax.ShapeDtypeStruct((LEAVES, RHS, RANK), bf16),
            jax.ShapeDtypeStruct((LEAVES, RANK, 128), bf16),
            jax.ShapeDtypeStruct((LEAVES, ROWS, SIZE), bf16),
        ),
        in_specs=[VMEM] * 7 + [SMEM],
        out_specs=(VMEM,) * 4,
        scratch_shapes=[
            pltpu.VMEM((LEAVES, RHS, 128), bf16),
            pltpu.VMEM((LEAVES, 8, 128), f32),
            pltpu.VMEM((3, LEAVES, 128), f32),
            pltpu.VMEM((LEAVES, 128), f32),
        ],
        compiler_params=params(),
        name="prep",
    )(*operands)


def greet(me):
    barrier = pltpu.get_barrier_semaphore()

    def one(k, _):
        peer = lax.rem(me + k, PEERS)
        pl.semaphore_signal(barrier, inc=1, device_id=(peer // 4, lax.rem(peer, 4)), device_id_type=MESH)
        return 0

    lax.fori_loop(1, PEERS, one, 0)


def all_here():
    pl.semaphore_wait(pltpu.get_barrier_semaphore(), PEERS - 1)


def send_all(me, source, target, send_sem, recv_sem, own_sem):
    pltpu.make_async_copy(source.at[me], target.at[me], own_sem).start()

    def one(k, _):
        peer = lax.rem(me + k, PEERS)
        pltpu.make_async_remote_copy(
            src_ref=source.at[peer],
            dst_ref=target.at[me],
            send_sem=send_sem,
            recv_sem=recv_sem,
            device_id=(peer // 4, lax.rem(peer, 4)),
            device_id_type=MESH,
        ).start()
        return 0

    lax.fori_loop(1, PEERS, one, 0)


def wait_all(me, source, target, send_sem, recv_sem, own_sem):
    pltpu.make_async_copy(source.at[me], target.at[me], own_sem).wait()
    most = pl.ds(0, PEERS - 1)
    pltpu.make_async_copy(source.at[most], source.at[most], send_sem).wait()
    pltpu.make_async_copy(target.at[most], target.at[most], recv_sem).wait()


class Near:
    def __init__(self, vec, cnt, acc, left_t, right_t, ks, kt, va):
        self.vec, self.cnt, self.acc, self.left_t, self.right_t = vec, cnt, acc, left_t, right_t
        self.ks, self.kt, self.va = ks, kt, va

    def features(self, j, tile):
        self.vec[j] = tile[0:32, :]
        rows = tile[32:48, :].astype(f32)
        left, right = point_features((rows[0:1], rows[1:2], rows[2:3]))
        self.right_t[j] = stack_rows(right, 16, SIZE).astype(bf16)
        self.left_t[j] = stack_rows(left, 128, SIZE).T.astype(bf16)
        self.cnt[j] = rows[3:4, 0:128]

    def make(self, j, at):
        right = self.right_t[j]
        for b in range(BAND):
            v = jnp.dot(self.left_t[j - REACH + b, :, 0:16], right, preferred_element_type=f32)
            k = kappa(v)
            self.ks[at][b * SIZE : (b + 1) * SIZE, :] = k
            if b < REACH:
                self.kt[at][b * SIZE : (b + 1) * SIZE, :] = k.T

    def apply(self, j, at):
        ks, kt, va, acc = self.ks[at], self.kt[at], self.va[at], self.acc
        vj = self.vec[j]
        cj = self.cnt[j]

        def spread(c):
            c = jnp.broadcast_to(c, (RHS, 128)).astype(bf16)
            return jnp.concatenate([c, c], axis=1)

        for b in range(BAND):
            i = j - REACH + b
            d = REACH - b
            ahead = spread(self.cnt[i][:, REACH + d : REACH + d + 1])
            behind = spread(cj[:, REACH - d : REACH - d + 1])
            vi = self.vec[i]
            cols = slice(b * SIZE, (b + 1) * SIZE)
            va[0:16, cols] = vi[0:16] * behind
            va[16:32, cols] = vi[16:32] * ahead
            if b < REACH:
                vb = jnp.concatenate([vj[0:16] * ahead, vj[16:32] * behind], axis=0)
                acc[i] += jnp.dot(vb, kt[cols, :], preferred_element_type=f32)
        twice = jnp.broadcast_to(cj[:, REACH : REACH + 1] * NUGGET, (2 * RHS, 128))
        twice = jnp.concatenate([twice, twice], axis=1)
        acc[j] += jnp.dot(va[...], ks[...], preferred_element_type=f32) + twice * vj.astype(f32)


NEAR_SCRATCH = [
    pltpu.VMEM((EXT, 2 * RHS, SIZE), bf16),
    pltpu.VMEM((EXT, 1, 128), f32),
    pltpu.VMEM((EXT, 2 * RHS, SIZE), f32),
    pltpu.VMEM((EXT, SIZE, 128), bf16),
    pltpu.VMEM((EXT, 16, SIZE), bf16),
    pltpu.VMEM((BAND * SIZE, SIZE), bf16),
    pltpu.VMEM((BAND * SIZE, SIZE), bf16),
    pltpu.VMEM((BAND * SIZE, SIZE), bf16),
    pltpu.VMEM((BAND * SIZE, SIZE), bf16),
    pltpu.VMEM((2 * RHS, BAND * SIZE), bf16),
    pltpu.VMEM((2 * RHS, BAND * SIZE), bf16),
]


def near_first_kernel(
    block, payload, block_far, out, arrived, halo, vec, cnt, acc, left_t, right_t, ks0, ks1, kt0, kt1, va0, va1,
    send_sem, recv_sem, own_sem, edge_send, edge_recv
):
    me = device_id()
    greet(me)
    near = Near(vec, cnt, acc, left_t, right_t, (ks0, ks1), (kt0, kt1), (va0, va1))
    acc[...] = jnp.zeros_like(acc)

    def first(j, _):
        near.features(j + REACH, block[j])
        return 0

    lax.fori_loop(0, REACH + FIRST_COLUMNS, first, 0, unroll=4)
    begin = 2 * REACH
    near.make(begin, 0)
    all_here()
    edges = []
    for side in range(2):
        peer = lax.rem(me + (1 if side == 0 else PEERS - 1), PEERS)
        rows = pl.ds(LEAVES - REACH, REACH) if side == 0 else pl.ds(0, REACH)
        edges.append(
            pltpu.make_async_remote_copy(
                src_ref=block_far.at[rows],
                dst_ref=halo.at[pl.ds(side * REACH, REACH)],
                send_sem=edge_send.at[side],
                recv_sem=edge_recv.at[side],
                device_id=(peer // 4, lax.rem(peer, 4)),
                device_id_type=MESH,
            )
        )
        edges[-1].start()
    send_all(me, payload, arrived, send_sem, recv_sem, own_sem)

    def body(g, _):
        j = begin + 2 * g
        near.make(j + 1, 1)
        near.apply(j, 0)
        near.make(j + 2, 0)
        near.apply(j + 1, 1)
        return 0

    lax.fori_loop(0, FIRST_COLUMNS // 2 - 1, body, 0)
    j = begin + FIRST_COLUMNS - 2
    near.make(j + 1, 1)
    near.apply(j, 0)
    near.apply(j + 1, 1)
    out[...] = acc[REACH : REACH + LEAVES]
    for edge in edges:
        edge.wait()
    wait_all(me, payload, arrived, send_sem, recv_sem, own_sem)


def near_first(block, payload):
    return pl.pallas_call(
        near_first_kernel,
        out_shape=(
            jax.ShapeDtypeStruct((LEAVES, 2 * RHS, SIZE), f32),
            jax.ShapeDtypeStruct((PEERS, RHS, 384), bf16),
            jax.ShapeDtypeStruct((2 * REACH, ROWS, SIZE), bf16),
        ),
        in_specs=[VMEM, ANY, ANY],
        out_specs=(VMEM, ANY, ANY),
        scratch_shapes=NEAR_SCRATCH
        + [pltpu.SemaphoreType.DMA] * 3
        + [pltpu.SemaphoreType.DMA((2,)), pltpu.SemaphoreType.DMA((2,))],
        compiler_params=params(collective_id=0, has_side_effects=True),
        name="near_first",
    )(block, payload, block)


def near_rest_kernel(
    block, halo, before, ret, out, came, vec, cnt, acc, left_t, right_t, ks0, ks1, kt0, kt1, va0, va1,
    send_sem, recv_sem, own_sem
):
    me = device_id()
    greet(me)
    near = Near(vec, cnt, acc, left_t, right_t, (ks0, ks1), (kt0, kt1), (va0, va1))

    def edge(j, _):
        near.features(j, halo[j])
        near.features(j + LEAVES + REACH, halo[j + REACH])
        acc[j] = jnp.zeros((2 * RHS, SIZE), f32)
        acc[j + LEAVES + REACH] = jnp.zeros((2 * RHS, SIZE), f32)
        return 0

    lax.fori_loop(0, REACH, edge, 0, unroll=2)

    def first(j, _):
        near.features(j + REACH, block[j])
        acc[j + REACH] = before[j]
        return 0

    lax.fori_loop(0, LEAVES, first, 0, unroll=4)
    begin = 2 * REACH + FIRST_COLUMNS
    upper = EXT - begin
    columns = upper + REACH

    def column(n):
        return jnp.where(n < upper, begin + n, n - upper + REACH)

    near.make(begin, 0)
    all_here()
    send_all(me, ret, came, send_sem, recv_sem, own_sem)

    def body(g, _):
        near.make(column(2 * g + 1), 1)
        near.apply(column(2 * g), 0)
        near.make(column(2 * g + 2), 0)
        near.apply(column(2 * g + 1), 1)
        return 0

    lax.fori_loop(0, columns // 2 - 1, body, 0)
    near.make(column(columns - 1), 1)
    near.apply(column(columns - 2), 0)
    near.apply(column(columns - 1), 1)
    out[...] = acc[REACH : REACH + LEAVES]
    wait_all(me, ret, came, send_sem, recv_sem, own_sem)


def near_rest(block, halo, before, ret):
    return pl.pallas_call(
        near_rest_kernel,
        out_shape=(
            jax.ShapeDtypeStruct((LEAVES, 2 * RHS, SIZE), f32),
            jax.ShapeDtypeStruct((PEERS, RHS, 256), bf16),
        ),
        in_specs=[VMEM, VMEM, VMEM, ANY],
        out_specs=(VMEM, ANY),
        scratch_shapes=NEAR_SCRATCH + [pltpu.SemaphoreType.DMA] * 3,
        compiler_params=params(collective_id=1, has_side_effects=True),
        name="near_rest",
    )(block, halo, before, ret)


def far_kernel(arrived, own, back, slot, far_in, ret, feat, coef, gt, ct0, ct1, ks0, ks1, acc_l, acc_u):
    ct, ks = (ct0, ct1), (ks0, ks1)
    low = lax.broadcasted_iota(jnp.int32, (RHS, 128), 1) < RANK
    low8 = lax.broadcasted_iota(jnp.int32, (8, 128), 1) < RANK
    tail = jnp.where(lax.broadcasted_iota(jnp.int32, (8, 128), 0) == 0, 1.0, 0.0).astype(f32)

    def both(x, mask):
        y = pltpu.roll(x, RANK, 1)
        return jnp.where(mask, x, y), jnp.where(mask, y, x)

    def table(d, _):
        for h in range(2):
            c = both(arrived[d, :, h * 128 : (h + 1) * 128].astype(f32), low)
            f = both(arrived[d, :, 256:384].astype(f32)[h * 8 : (h + 1) * 8], low8)
            for q in range(2):
                coef[d * CAP + 2 * h + q] = c[q].astype(bf16)
                feat[d * CAP + 2 * h + q] = jnp.concatenate([f[q], tail], axis=0).astype(bf16)
        return 0

    lax.fori_loop(0, PEERS, table, 0, unroll=4)
    acc_l[...] = jnp.zeros_like(acc_l)
    acc_u[...] = jnp.zeros_like(acc_u)

    def make(i, p):
        for m in range(FAR // 2):
            lanes = slice(m * 128, (m + 1) * 128)
            a, b = slot[i, 2 * m], slot[i, 2 * m + 1]
            gt[:, lanes] = jnp.where(low, feat[a], feat[b])
            ct[p][:, lanes] = jnp.where(low, coef[a], coef[b])
        mine = own[i, :, 0:16]
        for t in range(16):
            lanes = slice(t * 256, (t + 1) * 256)
            ks[p][:, lanes] = kappa(jnp.dot(mine, gt[:, lanes], preferred_element_type=f32))

    def apply(i, p):
        far_in[i] = lax.dot_general(ct[p][...], ks[p][...], NT, preferred_element_type=f32).astype(bf16)
        rt = jnp.dot(back[i], ks[p][...], preferred_element_type=f32)
        for m in range(FAR // 2):
            tile = rt[:, m * 128 : (m + 1) * 128]
            acc_l[slot[i, 2 * m]] += tile
            acc_u[slot[i, 2 * m + 1]] += tile

    make(0, 0)

    def pair(g, _):
        make(2 * g + 1, 1)
        apply(2 * g, 0)
        make(jnp.minimum(2 * g + 2, LEAVES - 1), 0)
        apply(2 * g + 1, 1)
        return 0

    lax.fori_loop(0, LEAVES // 2, pair, 0)

    def pack(d, _):
        for h in range(2):
            s = d * CAP + 2 * h
            even = acc_l[s] + pltpu.roll(acc_u[s], RANK, 1)
            odd = pltpu.roll(acc_l[s + 1], RANK, 1) + acc_u[s + 1]
            ret[d, :, h * 128 : (h + 1) * 128] = jnp.where(low, even, odd).astype(bf16)
        return 0

    lax.fori_loop(0, PEERS, pack, 0, unroll=4)


def far(arrived, own, back, slot):
    return pl.pallas_call(
        far_kernel,
        out_shape=(
            jax.ShapeDtypeStruct((LEAVES, RHS, RANK), bf16),
            jax.ShapeDtypeStruct((PEERS, RHS, 256), bf16),
        ),
        in_specs=[VMEM] * 3 + [SMEM],
        out_specs=(VMEM,) * 2,
        scratch_shapes=[
            pltpu.VMEM((SLOTS, 16, 128), bf16),
            pltpu.VMEM((SLOTS, RHS, 128), bf16),
            pltpu.VMEM((16, FAR * RANK), bf16),
            pltpu.VMEM((RHS, FAR * RANK), bf16),
            pltpu.VMEM((RHS, FAR * RANK), bf16),
            pltpu.VMEM((RANK, FAR * RANK), bf16),
            pltpu.VMEM((RANK, FAR * RANK), bf16),
            pltpu.VMEM((SLOTS, RHS, 128), f32),
            pltpu.VMEM((SLOTS, RHS, 128), f32),
        ],
        compiler_params=params(),
        name="far",
    )(arrived, own, back, slot)


def post_kernel(came, send, near_out, far_in, row_basis, col_basis, product, adjoint, acc_l, acc_u):
    acc_l[...] = jnp.zeros_like(acc_l)
    acc_u[...] = jnp.zeros_like(acc_u)

    def peer(d, _):
        for h in range(2):
            tile = came[d, :, h * 128 : (h + 1) * 128].astype(f32)
            acc_l[send[0, d, 2 * h]] += tile
            acc_u[send[0, d, 2 * h + 1]] += tile
        return 0

    lax.fori_loop(0, PEERS, peer, 0, unroll=4)

    def leaf(j, _):
        total = (acc_l[j] + pltpu.roll(acc_u[j], RANK, 1))[:, :RANK].astype(bf16)
        adjoint[j] = near_out[j, RHS:, :] + jnp.dot(total, col_basis[j], preferred_element_type=f32)
        product[j] = near_out[j, :RHS, :] + jnp.dot(far_in[j], row_basis[j], preferred_element_type=f32)
        return 0

    lax.fori_loop(0, LEAVES, leaf, 0, unroll=4)


def post(came, send, near_out, far_in, row_basis, col_basis):
    return pl.pallas_call(
        post_kernel,
        out_shape=(jax.ShapeDtypeStruct((LEAVES, RHS, SIZE), f32),) * 2,
        in_specs=[VMEM, SMEM] + [VMEM] * 4,
        out_specs=(VMEM,) * 2,
        scratch_shapes=[pltpu.VMEM((LEAVES, RHS, 128), f32)] * 2,
        compiler_params=params(),
        name="post",
    )(came, send, near_out, far_in, row_basis, col_basis)


def local(probe, weights, points, skeleton, row_basis, col_basis, near_leaf, far_slot, send_leaf):
    payload, back, own, block = prep(
        probe, weights, points, skeleton, row_basis, col_basis, near_leaf, send_leaf
    )
    near_part, arrived, halo = near_first(block, payload)
    far_in, ret = far(arrived, own, back, far_slot)
    near_out, came = near_rest(block, halo, near_part, ret)
    return post(came, send_leaf, near_out, far_in, row_basis, col_basis)


def solution(mesh):
    lead = P(("leaf", "sub"), None, None)
    flat = P(("leaf", "sub"), None)
    return jax.shard_map(
        local,
        mesh=mesh,
        in_specs=(lead, lead, lead, flat, lead, lead, flat, flat, lead),
        out_specs=(lead, lead),
        check_vma=False,
    )
```

time: 260 us -> 168 us (0.65)
  Pallas kernels: 191 us -> 162 us
  waiting for transfers between devices: 25.1 us -> 0 us
  starting transfers between devices: 22.8 us -> 0 us
  local copies, waits for them, and re-layouts: 17.4 us -> 4.42 us
    pallas_call x1, Pallas kernels: 62.7 us -> 45.5 us  [far(): pl.pallas_call(far_kernel, out_shape=(jax.ShapeDtypeStruct((LEAVES, RHS,...]
    all_to_all x2 -> x0, starting transfers between devices: 16.2 us -> none  [the longest x1 11.5 us: local(): lax.all_to_all(payload, axes, split_axis=0, concat_axis=0, tiled=True)]
    all_to_all x2 -> x0, waiting for transfers between devices: 13.5 us -> none  [the longest x1 13.5 us: local(): lax.all_to_all(payload, axes, split_axis=0, concat_axis=0, tiled=True)]
    ppermute x2 -> x0, waiting for transfers between devices: 11.5 us -> none  [the longest x1 9.83 us: local(): above = lax.ppermute(block[:REACH], axes, behind)]
    pallas_call x1, Pallas kernels: 20.6 us -> 10.3 us  [prep(): pl.pallas_call(prep_kernel, out_shape=(jax.ShapeDtypeStruct((PEERS, RHS,...]
    concatenate x1 -> x0, local copies, waits for them, and re-layouts: 9.9 us -> none  [local(): jnp.concatenate([probe, weights, points, counts[:, None, :], jnp.zeros((L...]
    pallas_call x1, Pallas kernels: 18.4 us -> 9.17 us  [post(): pl.pallas_call(post_kernel, out_shape=(jax.ShapeDtypeStruct((LEAVES, RHS,...]
    pallas_call x1 -> x2, Pallas kernels: 88.8 us -> 97.6 us  [the longest x1 56.6 us: near_rest(): pl.pallas_call(near_rest_kernel, out_shape=(jax.ShapeDtypeStruct((LEAVES,...]
  transfers between devices with their start and end apart: 4 -> 0, of which waited for: 3 -> 0; matrix products, arithmetic and copies ran while one was open for 5% -> 0% of each run, Pallas kernels for 34% -> 0%
where the time goes in v2:
time: 168 us
  Pallas kernels  162 us (96%)
  local copies, waits for them, and re-layouts  4.42 us (3%)
    pallas_call x1, Pallas kernels, near_rest(): pl.pallas_call(near_rest_kernel, out_shape=(jax.ShapeDtypeStruct((LEAVES,...  56.6 us
    pallas_call x1, Pallas kernels, far(): pl.pallas_call(far_kernel, out_shape=(jax.ShapeDtypeStruct((LEAVES, RHS,...  45.5 us
    pallas_call x1, Pallas kernels, near_first(): pl.pallas_call(near_first_kernel, out_shape=(jax.ShapeDtypeStruct((LEAVES...  40.9 us
    pallas_call x1, Pallas kernels, prep(): pl.pallas_call(prep_kernel, out_shape=(jax.ShapeDtypeStruct((PEERS, RHS,...  10.3 us
    pallas_call x1, Pallas kernels, post(): pl.pallas_call(post_kernel, out_shape=(jax.ShapeDtypeStruct((LEAVES, RHS,...  9.17 us
    unnamed x3, local copies, waits for them, and re-layouts  4.42 us

profile of v2, /device:TPU:1, one launch (start us, length us, event | category | flops | bytes accessed | tf_op | source)
XLA Modules:
  0.0 167.5 jit_solution(4674989943100766199)
XLA Ops:
  0.6 1.4 copy.12.near_leaf
  2.0 1.4 copy.13.send
  3.4 1.6 copy.11.points
  5.0 10.3 %prep.1 = (bf16[128,16,384]{2,1,0:T(8,128)(2,1)}, bf16[64,16,64]{2,1,0:T(8,128)(2,1)}, bf16[64,64,128]{2,1,0:T(8,128)(2,1)}, bf16[64,48,256]{2,1,0:T(8,128)(2,1)}) custom-call(bf16[64,16,256]{2,1,0:T(8,128)(2,1)} %probe.1, bf16[64,16,256]{2,1,0:T(8,128)(2,1)} %weights.1, bf16[64,3,256]{2,1,0:T(4,128)(2,1)} %copy.11.points, bf16[64,192]{1,0:T(8,128)(2,1)} %skeleton.1, ...), custom_call_target="tpu_custom_call" | custom-call | tf_op jit(solution)/shard_map/prep/pallas_call | solution.py:120
  15.3 40.9 %near_first.1 = (f32[64,32,256]{2,1,0:T(8,128)}, bf16[128,16,384]{2,1,0:T(8,128)(2,1)}, bf16[16,48,256]{2,1,0:T(8,128)(2,1)}) custom-call(bf16[64,48,256]{2,1,0:T(8,128)(2,1)} %get-tuple-element.13.block.block_far, bf16[128,16,384]{2,1,0:T(8,128)(2,1)} %get-tuple-element.14.payload, bf16[64,48,256]{2,1,0:T(8,128)(2,1)} %get-tuple-element.13.block.block_far), custom_call_target="tpu_custom_call" | custom-call | tf_op jit(solution)/shard_map/near_first/pallas_call | solution.py:298
  56.3 45.5 %far.1 = (bf16[64,16,64]{2,1,0:T(8,128)(2,1)}, bf16[128,16,256]{2,1,0:T(8,128)(2,1)}) custom-call(bf16[128,16,384]{2,1,0:T(8,128)(2,1)} %get-tuple-element.17.arrived, bf16[64,64,128]{2,1,0:T(8,128)(2,1)} %get-tuple-element.18.own, bf16[64,16,64]{2,1,0:T(8,128)(2,1)} %get-tuple-element.19.back, s32[64,64]{1,0:T(8,128)} %slot.1), custom_call_target="tpu_custom_call" | custom-call | tf_op jit(solution)/shard_map/far/pallas_call | solution.py:444
  101.7 56.6 %near_rest.1 = (f32[64,32,256]{2,1,0:T(8,128)}, bf16[128,16,256]{2,1,0:T(8,128)(2,1)}) custom-call(bf16[64,48,256]{2,1,0:T(8,128)(2,1)} %get-tuple-element.13.block.block_far, bf16[16,48,256]{2,1,0:T(8,128)(2,1)} %get-tuple-element.15.halo, f32[64,32,256]{2,1,0:T(8,128)} %get-tuple-element.16.before, bf16[128,16,256]{2,1,0:T(8,128)(2,1)} %get-tuple-element.20.ret), custom_call_target="tpu_custom_call" | custom-call | tf_op jit(solution)/shard_map/near_rest/pallas_call | solution.py:365
  158.4 9.2 %post.1 = (f32[64,16,256]{2,1,0:T(8,128)}, f32[64,16,256]{2,1,0:T(8,128)}) custom-call(bf16[128,16,256]{2,1,0:T(8,128)(2,1)} %get-tuple-element.21.came, s32[1,128,4]{2,1,0:T(8,128)} %copy.13.send, f32[64,32,256]{2,1,0:T(8,128)} %get-tuple-element.22.near_out, bf16[64,16,64]{2,1,0:T(8,128)(2,1)} %get-tuple-element.23.far_in, bf16[64,64,256]{2,1,0:T(8,128)(2,1)} %row_basis.3, ...), custom_call_target="tpu_custom_call" | custom-call | tf_op jit(solution)/shard_map/post/pallas_call | solution.py:491

commit v3 on v2

--- a/solution.py
+++ b/solution.py
@@ -33,7 +33,7 @@
 SMEM = pl.BlockSpec(memory_space=pltpu.SMEM)
 
 
-def params(mib=60, **more):
+def params(mib=24, **more):
     return pltpu.CompilerParams(vmem_limit_bytes=mib * 2**20, **more)
 
 
@@ -70,7 +70,7 @@
 
 
 def prep_kernel(
-    probe, weights, points, skeleton, row_basis, col_basis, near_leaf, send, out, back, own, block, coef_t, feat_t, sk, cnt
+    probe, weights, points, skeleton, row_basis, col_basis, near_leaf, send, out, back, own, block, coef_t, feat_t, sk, cnt, pts
 ):
     low = lax.broadcasted_iota(jnp.int32, (RHS, 128), 1) < RANK
     low8 = lax.broadcasted_iota(jnp.int32, (8, 128), 1) < RANK
@@ -81,12 +81,16 @@
     sk[1] = jnp.where(low64, yx, xy)
     z = skeleton[:, 128:192].astype(f32)
     sk[2] = jnp.concatenate([z, z], axis=1)
-    ids = device_id() * LEAVES + lax.broadcasted_iota(jnp.int32, (LEAVES, 128), 0)
-    target = ids + lax.broadcasted_iota(jnp.int32, (LEAVES, 128), 1) - REACH
-    total = jnp.zeros((LEAVES, 128), f32)
-    for m in range(near_leaf.shape[1]):
-        total = total + jnp.where(near_leaf[:, m : m + 1] == target, 1.0, 0.0)
-    cnt[...] = jnp.where(lax.broadcasted_iota(jnp.int32, (LEAVES, 128), 1) <= 2 * REACH, total, 0.0)
+    ids = device_id() * LEAVES + lax.broadcasted_iota(jnp.int32, (32, LEAVES), 1)
+    offset = lax.broadcasted_iota(jnp.int32, (32, LEAVES), 0)
+    total = jnp.zeros((32, LEAVES), f32)
+    for m in range(near_leaf.shape[0]):
+        total = total + jnp.where(near_leaf[m : m + 1, :] == ids + (offset - REACH), 1.0, 0.0)
+    total = jnp.where(offset <= 2 * REACH, total, 0.0)
+    total = jnp.concatenate([total, total], axis=1)
+    cnt[...] = jnp.concatenate([total, jnp.zeros((96, 128), f32)], axis=0).T[0:LEAVES]
+    for c in range(3):
+        pts[c] = points[c].astype(f32)
 
     def leaf(j, _):
         c = lax.dot_general(probe[j], col_basis[j], NT, preferred_element_type=f32)
@@ -97,16 +101,15 @@
         own[j] = stack_rows(left, 128, 128)[:, :RANK].T.astype(bf16)
         block[j, 0:16, :] = probe[j]
         block[j, 16:32, :] = weights[j]
-        p = points[j].astype(f32)
         n = cnt[pl.ds(j, 1), :]
-        rows = [p[0:1], p[1:2], p[2:3], jnp.concatenate([n, jnp.zeros((1, 128), f32)], axis=1)]
+        rows = [*(pts[c, pl.ds(j, 1), :] for c in range(3)), jnp.concatenate([n, jnp.zeros((1, 128), f32)], axis=1)]
         block[j, 32:48, :] = stack_rows(rows, 16, SIZE).astype(bf16)
         return 0
 
     lax.fori_loop(0, LEAVES, leaf, 0, unroll=4)
 
     def peer(d, _):
-        at = [send[0, d, q] for q in range(CAP)]
+        at = [send[q, d] for q in range(CAP)]
         for h in range(2):
             out[d, :, h * 128 : (h + 1) * 128] = jnp.where(low, coef_t[at[2 * h]], coef_t[at[2 * h + 1]])
         f = [jnp.where(low8, feat_t[at[2 * h]], feat_t[at[2 * h + 1]]) for h in range(2)]
@@ -132,6 +135,7 @@
             pltpu.VMEM((LEAVES, 8, 128), f32),
             pltpu.VMEM((3, LEAVES, 128), f32),
             pltpu.VMEM((LEAVES, 128), f32),
+            pltpu.VMEM((3, LEAVES, SIZE), f32),
         ],
         compiler_params=params(),
         name="prep",
@@ -191,29 +195,32 @@
         self.left_t[j] = stack_rows(left, 128, SIZE).T.astype(bf16)
         self.cnt[j] = rows[3:4, 0:128]
 
-    def make(self, j, at):
-        right = self.right_t[j]
+    def make(self, j, at, b):
+        v = jnp.dot(self.left_t[j - REACH + b, :, 0:16], self.right_t[j], preferred_element_type=f32)
+        k = kappa(v)
+        self.ks[at][b * SIZE : (b + 1) * SIZE, :] = k
+        if b < REACH:
+            self.kt[at][b * SIZE : (b + 1) * SIZE, :] = k.T
+
+    def make_all(self, j, at):
         for b in range(BAND):
-            v = jnp.dot(self.left_t[j - REACH + b, :, 0:16], right, preferred_element_type=f32)
-            k = kappa(v)
-            self.ks[at][b * SIZE : (b + 1) * SIZE, :] = k
-            if b < REACH:
-                self.kt[at][b * SIZE : (b + 1) * SIZE, :] = k.T
-
-    def apply(self, j, at):
+            self.make(j, at, b)
+
+    def step(self, j, at, j_next=None):
         ks, kt, va, acc = self.ks[at], self.kt[at], self.va[at], self.acc
         vj = self.vec[j]
         cj = self.cnt[j]
 
-        def spread(c):
-            c = jnp.broadcast_to(c, (RHS, 128)).astype(bf16)
+        def spread(c, rows=RHS):
+            c = jnp.broadcast_to(c, (rows, 128))
             return jnp.concatenate([c, c], axis=1)
 
+        total = spread(cj[:, REACH : REACH + 1] * NUGGET, 2 * RHS) * vj.astype(f32)
         for b in range(BAND):
             i = j - REACH + b
             d = REACH - b
-            ahead = spread(self.cnt[i][:, REACH + d : REACH + d + 1])
-            behind = spread(cj[:, REACH - d : REACH - d + 1])
+            ahead = spread(self.cnt[i][:, REACH + d : REACH + d + 1]).astype(bf16)
+            behind = spread(cj[:, REACH - d : REACH - d + 1]).astype(bf16)
             vi = self.vec[i]
             cols = slice(b * SIZE, (b + 1) * SIZE)
             va[0:16, cols] = vi[0:16] * behind
@@ -221,9 +228,12 @@
             if b < REACH:
                 vb = jnp.concatenate([vj[0:16] * ahead, vj[16:32] * behind], axis=0)
                 acc[i] += jnp.dot(vb, kt[cols, :], preferred_element_type=f32)
-        twice = jnp.broadcast_to(cj[:, REACH : REACH + 1] * NUGGET, (2 * RHS, 128))
-        twice = jnp.concatenate([twice, twice], axis=1)
-        acc[j] += jnp.dot(va[...], ks[...], preferred_element_type=f32) + twice * vj.astype(f32)
+            if b % 3 == 2:
+                cols = slice((b - 2) * SIZE, (b + 1) * SIZE)
+                total = total + jnp.dot(va[:, cols], ks[cols, :], preferred_element_type=f32)
+            if j_next is not None:
+                self.make(j_next, 1 - at, b)
+        acc[j] += total
 
 
 NEAR_SCRATCH = [
@@ -256,7 +266,7 @@
 
     lax.fori_loop(0, REACH + FIRST_COLUMNS, first, 0, unroll=4)
     begin = 2 * REACH
-    near.make(begin, 0)
+    near.make_all(begin, 0)
     all_here()
     edges = []
     for side in range(2):
@@ -277,17 +287,14 @@
 
     def body(g, _):
         j = begin + 2 * g
-        near.make(j + 1, 1)
-        near.apply(j, 0)
-        near.make(j + 2, 0)
-        near.apply(j + 1, 1)
+        near.step(j, 0, j + 1)
+        near.step(j + 1, 1, j + 2)
         return 0
 
     lax.fori_loop(0, FIRST_COLUMNS // 2 - 1, body, 0)
     j = begin + FIRST_COLUMNS - 2
-    near.make(j + 1, 1)
-    near.apply(j, 0)
-    near.apply(j + 1, 1)
+    near.step(j, 0, j + 1)
+    near.step(j + 1, 1)
     out[...] = acc[REACH : REACH + LEAVES]
     for edge in edges:
         edge.wait()
@@ -342,21 +349,18 @@
     def column(n):
         return jnp.where(n < upper, begin + n, n - upper + REACH)
 
-    near.make(begin, 0)
+    near.make_all(begin, 0)
     all_here()
     send_all(me, ret, came, send_sem, recv_sem, own_sem)
 
     def body(g, _):
-        near.make(column(2 * g + 1), 1)
-        near.apply(column(2 * g), 0)
-        near.make(column(2 * g + 2), 0)
-        near.apply(column(2 * g + 1), 1)
+        near.step(column(2 * g), 0, column(2 * g + 1))
+        near.step(column(2 * g + 1), 1, column(2 * g + 2))
         return 0
 
     lax.fori_loop(0, columns // 2 - 1, body, 0)
-    near.make(column(columns - 1), 1)
-    near.apply(column(columns - 2), 0)
-    near.apply(column(columns - 1), 1)
+    near.step(column(columns - 2), 0, column(columns - 1))
+    near.step(column(columns - 1), 1)
     out[...] = acc[REACH : REACH + LEAVES]
     wait_all(me, ret, came, send_sem, recv_sem, own_sem)
 
@@ -376,8 +380,8 @@
     )(block, halo, before, ret)
 
 
-def far_kernel(arrived, own, back, slot, far_in, ret, feat, coef, gt, ct0, ct1, ks0, ks1, acc_l, acc_u):
-    ct, ks = (ct0, ct1), (ks0, ks1)
+def far_kernel(arrived, own, back, slot, far_in, ret, feat, coef, gt0, gt1, ct0, ct1, ks0, ks1, acc_l, acc_u):
+    gt, ct, ks = (gt0, gt1), (ct0, ct1), (ks0, ks1)
     low = lax.broadcasted_iota(jnp.int32, (RHS, 128), 1) < RANK
     low8 = lax.broadcasted_iota(jnp.int32, (8, 128), 1) < RANK
     tail = jnp.where(lax.broadcasted_iota(jnp.int32, (8, 128), 0) == 0, 1.0, 0.0).astype(f32)
@@ -399,32 +403,47 @@
     acc_l[...] = jnp.zeros_like(acc_l)
     acc_u[...] = jnp.zeros_like(acc_u)
 
-    def make(i, p):
-        for m in range(FAR // 2):
+    def gather(i, p, t):
+        for m in range(2 * t, 2 * t + 2):
             lanes = slice(m * 128, (m + 1) * 128)
             a, b = slot[i, 2 * m], slot[i, 2 * m + 1]
-            gt[:, lanes] = jnp.where(low, feat[a], feat[b])
+            gt[p][:, lanes] = jnp.where(low, feat[a], feat[b])
             ct[p][:, lanes] = jnp.where(low, coef[a], coef[b])
-        mine = own[i, :, 0:16]
-        for t in range(16):
-            lanes = slice(t * 256, (t + 1) * 256)
-            ks[p][:, lanes] = kappa(jnp.dot(mine, gt[:, lanes], preferred_element_type=f32))
-
-    def apply(i, p):
-        far_in[i] = lax.dot_general(ct[p][...], ks[p][...], NT, preferred_element_type=f32).astype(bf16)
-        rt = jnp.dot(back[i], ks[p][...], preferred_element_type=f32)
-        for m in range(FAR // 2):
+
+    def make(i, p, t):
+        lanes = slice(t * 256, (t + 1) * 256)
+        ks[p][:, lanes] = kappa(jnp.dot(own[i, :, 0:16], gt[p][:, lanes], preferred_element_type=f32))
+
+    def apply(i, p, t, w):
+        lanes = slice(t * 256, (t + w) * 256)
+        part = lax.dot_general(ct[p][:, lanes], ks[p][:, lanes], NT, preferred_element_type=f32)
+        rt = jnp.dot(back[i], ks[p][:, lanes], preferred_element_type=f32)
+        for m in range(2 * w):
             tile = rt[:, m * 128 : (m + 1) * 128]
-            acc_l[slot[i, 2 * m]] += tile
-            acc_u[slot[i, 2 * m + 1]] += tile
-
-    make(0, 0)
+            acc_l[slot[i, 4 * t + 2 * m]] += tile
+            acc_u[slot[i, 4 * t + 2 * m + 1]] += tile
+        return part
+
+    TILES = 16
+    W = 2
+
+    def step(i_next, p_next, i, p):
+        total = None
+        for t in range(0, TILES, W):
+            part = apply(i, p, t, W)
+            total = part if total is None else total + part
+            for u in range(t, t + W):
+                gather(i_next, p_next, u)
+                make(i_next, p_next, u)
+        far_in[i] = total.astype(bf16)
+
+    for t in range(TILES):
+        gather(0, 0, t)
+        make(0, 0, t)
 
     def pair(g, _):
-        make(2 * g + 1, 1)
-        apply(2 * g, 0)
-        make(jnp.minimum(2 * g + 2, LEAVES - 1), 0)
-        apply(2 * g + 1, 1)
+        step(2 * g + 1, 1, 2 * g, 0)
+        step(jnp.minimum(2 * g + 2, LEAVES - 1), 0, 2 * g + 1, 1)
         return 0
 
     lax.fori_loop(0, LEAVES // 2, pair, 0)
@@ -453,6 +472,7 @@
             pltpu.VMEM((SLOTS, 16, 128), bf16),
             pltpu.VMEM((SLOTS, RHS, 128), bf16),
             pltpu.VMEM((16, FAR * RANK), bf16),
+            pltpu.VMEM((16, FAR * RANK), bf16),
             pltpu.VMEM((RHS, FAR * RANK), bf16),
             pltpu.VMEM((RHS, FAR * RANK), bf16),
             pltpu.VMEM((RANK, FAR * RANK), bf16),
@@ -472,8 +492,8 @@
     def peer(d, _):
         for h in range(2):
             tile = came[d, :, h * 128 : (h + 1) * 128].astype(f32)
-            acc_l[send[0, d, 2 * h]] += tile
-            acc_u[send[0, d, 2 * h + 1]] += tile
+            acc_l[send[2 * h, d]] += tile
+            acc_u[send[2 * h + 1, d]] += tile
         return 0
 
     lax.fori_loop(0, PEERS, peer, 0, unroll=4)
@@ -500,13 +520,14 @@
 
 
 def local(probe, weights, points, skeleton, row_basis, col_basis, near_leaf, far_slot, send_leaf):
+    send = send_leaf.transpose(0, 2, 1).reshape(CAP, PEERS)
     payload, back, own, block = prep(
-        probe, weights, points, skeleton, row_basis, col_basis, near_leaf, send_leaf
+        probe, weights, points.transpose(1, 0, 2), skeleton, row_basis, col_basis, near_leaf.T, send
     )
     near_part, arrived, halo = near_first(block, payload)
     far_in, ret = far(arrived, own, back, far_slot)
     near_out, came = near_rest(block, halo, near_part, ret)
-    return post(came, send_leaf, near_out, far_in, row_basis, col_basis)
+    return post(came, send, near_out, far_in, row_basis, col_basis)
 
 
 def solution(mesh):

time: 168 us -> 143 us (0.85)
  Pallas kernels: 162 us -> 134 us
  local copies, waits for them, and re-layouts: 4.42 us -> 8.31 us
    pallas_call x1, Pallas kernels: 56.6 us -> 46.5 us  [near_rest(): pl.pallas_call(near_rest_kernel, out_shape=(jax.ShapeDtypeStruct((LEAVES,...]
    pallas_call x1, Pallas kernels: 45.5 us -> 37.3 us  [far(): pl.pallas_call(far_kernel, out_shape=(jax.ShapeDtypeStruct((LEAVES, RHS,...]
    pallas_call x1, Pallas kernels: 10.3 us -> 6.24 us  [prep(): pl.pallas_call(prep_kernel, out_shape=(jax.ShapeDtypeStruct((PEERS, RHS,...]
    unnamed x3 -> x24, local copies, waits for them, and re-layouts: 4.42 us -> 8.31 us
    pallas_call x1, Pallas kernels: 40.9 us -> 37.2 us  [near_first(): pl.pallas_call(near_first_kernel, out_shape=(jax.ShapeDtypeStruct((LEAVES...]
    pallas_call x1, Pallas kernels: 9.17 us -> 6.61 us  [post(): pl.pallas_call(post_kernel, out_shape=(jax.ShapeDtypeStruct((LEAVES, RHS,...]
where the time goes in v3:
time: 143 us
  Pallas kernels  134 us (94%)
  local copies, waits for them, and re-layouts  8.31 us (6%)
    pallas_call x1, Pallas kernels, near_rest(): pl.pallas_call(near_rest_kernel, out_shape=(jax.ShapeDtypeStruct((LEAVES,...  46.5 us
    pallas_call x1, Pallas kernels, far(): pl.pallas_call(far_kernel, out_shape=(jax.ShapeDtypeStruct((LEAVES, RHS,...  37.3 us
    pallas_call x1, Pallas kernels, near_first(): pl.pallas_call(near_first_kernel, out_shape=(jax.ShapeDtypeStruct((LEAVES...  37.2 us
    unnamed x24, local copies, waits for them, and re-layouts  8.31 us
    pallas_call x1, Pallas kernels, post(): pl.pallas_call(post_kernel, out_shape=(jax.ShapeDtypeStruct((LEAVES, RHS,...  6.61 us
    pallas_call x1, Pallas kernels, prep(): pl.pallas_call(prep_kernel, out_shape=(jax.ShapeDtypeStruct((PEERS, RHS,...  6.24 us

profile of v3, /device:TPU:1, one launch (start us, length us, event | category | flops | bytes accessed | tf_op | source)
XLA Modules:
  0.0 142.9 jit_solution(16064890807079773115)
XLA Ops:
  0.6 0.0 copy-start
  0.6 1.6 %copy-done = bf16[64,64,256]{2,1,0:T(8,128)(2,1)S(1)} copy-done((bf16[64,64,256]{2,1,0:T(8,128)(2,1)S(1)}, bf16[64,64,256]{2,1,0:T(8,128)(2,1)}, u32[]{:S(2)}) %copy-start) | copy-done | bytes 2097176
  2.2 0.0 copy-start.2
  2.2 1.6 %copy-done.2 = bf16[64,64,256]{2,1,0:T(8,128)(2,1)S(1)} copy-done((bf16[64,64,256]{2,1,0:T(8,128)(2,1)S(1)}, bf16[64,64,256]{2,1,0:T(8,128)(2,1)}, u32[]{:S(2)}) %copy-start.2) | copy-done | bytes 2097176
  3.8 0.0 copy-start.4
  3.8 1.0 copy-done.4
  4.9 0.0 copy-start.5
  4.9 1.0 copy-done.5
  5.9 0.0 copy-start.6
  5.9 0.9 copy-done.6
  6.8 0.0 copy-start.7
  6.8 0.8 copy-done.7
  7.6 0.0 copy-start.9
  7.6 0.7 copy-done.9
  8.2 0.0 copy-start.11
  8.2 0.7 copy-done.11
  8.9 6.2 %prep.1 = (bf16[128,16,384]{2,1,0:T(8,128)(2,1)S(1)}, bf16[64,16,64]{2,1,0:T(8,128)(2,1)S(1)}, bf16[64,64,128]{2,1,0:T(8,128)(2,1)S(1)}, bf16[64,48,256]{2,1,0:T(8,128)(2,1)S(1)}) custom-call(bf16[64,16,256]{2,1,0:T(8,128)(2,1)S(1)} %copy-done.4, bf16[64,16,256]{2,1,0:T(8,128)(2,1)S(1)} %copy-done.5, bf16[3,64,256]{2,1,0:T(8,128)(2,1)S(1)} %bitcast.5, ...), custom_call_target="tpu_custom_call" | custom-call | tf_op jit(solution)/shard_map/prep/pallas_call | solution.py:123
  15.2 0.0 copy-start.8
  15.2 37.2 %near_first.1 = (f32[64,32,256]{2,1,0:T(8,128)S(1)}, bf16[128,16,384]{2,1,0:T(8,128)(2,1)S(1)}, bf16[16,48,256]{2,1,0:T(8,128)(2,1)S(1)}) custom-call(bf16[64,48,256]{2,1,0:T(8,128)(2,1)S(1)} %get-tuple-element.13.block.block_far, bf16[128,16,384]{2,1,0:T(8,128)(2,1)S(1)} %get-tuple-element.14.payload, bf16[64,48,256]{2,1,0:T(8,128)(2,1)S(1)} %get-tuple-element.13.block.block_far), custom_call_target="tpu_custom_call" | custom-call | tf_op jit(solution)/shard_map/near_first/pallas_call | solution.py:305
  52.4 0.0 copy-done.8
  52.4 37.3 %far.1 = (bf16[64,16,64]{2,1,0:T(8,128)(2,1)S(1)}, bf16[128,16,256]{2,1,0:T(8,128)(2,1)S(1)}) custom-call(bf16[128,16,384]{2,1,0:T(8,128)(2,1)S(1)} %get-tuple-element.17.arrived, bf16[64,64,128]{2,1,0:T(8,128)(2,1)S(1)} %get-tuple-element.18.own, bf16[64,16,64]{2,1,0:T(8,128)(2,1)S(1)} %get-tuple-element.19.back, s32[64,64]{1,0:T(8,128)S(1)} %copy-done.8), custom_call_target="tpu_custom_call" | custom-call | tf_op jit(solution)/shard_map/far/pallas_call | solution.py:463
  89.7 0.0 copy-start.1
  89.7 0.0 copy-start.3
  89.7 0.0 copy-start.10
  89.7 46.5 %near_rest.1 = (f32[64,32,256]{2,1,0:T(8,128)S(1)}, bf16[128,16,256]{2,1,0:T(8,128)(2,1)S(1)}) custom-call(bf16[64,48,256]{2,1,0:T(8,128)(2,1)S(1)} %get-tuple-element.13.block.block_far, bf16[16,48,256]{2,1,0:T(8,128)(2,1)S(1)} %get-tuple-element.15.halo, f32[64,32,256]{2,1,0:T(8,128)S(1)} %get-tuple-element.16.before, ...), custom_call_target="tpu_custom_call" | custom-call | tf_op jit(solution)/shard_map/near_rest/pallas_call | solution.py:369
  136.3 0.0 copy-done.1
  136.3 0.0 copy-done.3
  136.3 0.0 copy-done.10
  136.3 6.6 %post.1 = (f32[64,16,256]{2,1,0:T(8,128)}, f32[64,16,256]{2,1,0:T(8,128)}) custom-call(bf16[128,16,256]{2,1,0:T(8,128)(2,1)S(1)} %get-tuple-element.21.came, s32[4,128]{1,0:T(4,128)S(1)} %bitcast.7, f32[64,32,256]{2,1,0:T(8,128)S(1)} %get-tuple-element.22.near_out, bf16[64,16,64]{2,1,0:T(8,128)(2,1)S(1)} %get-tuple-element.23.far_in, ...), custom_call_target="tpu_custom_call" | custom-call | tf_op jit(solution)/shard_map/post/pallas_call | solution.py:511
Async XLA Ops:
  0.6 1.6 %copy-start = (bf16[64,64,256]{2,1,0:T(8,128)(2,1)S(1)}, bf16[64,64,256]{2,1,0:T(8,128)(2,1)}, u32[]{:S(2)}) copy-start(bf16[64,64,256]{2,1,0:T(8,128)(2,1)} %row_basis.3) | copy-start | bytes 6291460
  2.2 1.6 %copy-start.2 = (bf16[64,64,256]{2,1,0:T(8,128)(2,1)S(1)}, bf16[64,64,256]{2,1,0:T(8,128)(2,1)}, u32[]{:S(2)}) copy-start(bf16[64,64,256]{2,1,0:T(8,128)(2,1)} %col_basis.3) | copy-start | bytes 6291460
  3.8 1.0 copy-start.4
  4.9 1.0 copy-start.5
  5.9 0.9 copy-start.6
  6.8 0.8 copy-start.7
  7.6 0.7 copy-start.9
  8.2 0.7 copy-start.11
  15.2 37.2 %copy-start.8 = (s32[64,64]{1,0:T(8,128)S(1)}, s32[64,64]{1,0:T(8,128)}, u32[]{:S(2)}) copy-start(s32[64,64]{1,0:T(8,128)} %slot.1) | copy-start | bytes 49156
  89.7 46.6 %copy-start.1 = (bf16[64,64,256]{2,1,0:T(8,128)(2,1)S(1)}, bf16[64,64,256]{2,1,0:T(8,128)(2,1)}, u32[]{:S(2)}) copy-start(bf16[64,64,256]{2,1,0:T(8,128)(2,1)} %row_basis.3) | copy-start | bytes 6291460
  89.7 46.6 %copy-start.3 = (bf16[64,64,256]{2,1,0:T(8,128)(2,1)S(1)}, bf16[64,64,256]{2,1,0:T(8,128)(2,1)}, u32[]{:S(2)}) copy-start(bf16[64,64,256]{2,1,0:T(8,128)(2,1)} %col_basis.3) | copy-start | bytes 6291460
  89.7 46.6 %copy-start.10 = (s32[1,128,4]{1,2,0:T(4,128)S(1)}, s32[1,128,4]{1,2,0:T(4,128)}, u32[]{:S(2)}) copy-start(s32[1,128,4]{1,2,0:T(4,128)} %param.17) | copy-start | bytes 6148

commit v4 on v3

--- a/solution.py
+++ b/solution.py
@@ -19,6 +19,7 @@
 SIZE = 256
 RANK = 64
 CAP = 4
+PREP_MIB = 54
 PEERS = 128
 SLOTS = PEERS * CAP
 FAR = 64
@@ -27,9 +28,10 @@
 NT = (((1,), (1,)), ((), ()))
 MESH = pl.DeviceIdType.MESH
 ROWS = 48
-FIRST_COLUMNS = 28
+FIRST_COLUMNS = 40
 VMEM = pl.BlockSpec(memory_space=pltpu.VMEM)
 ANY = pl.BlockSpec(memory_space=pl.ANY)
+HBM = pl.BlockSpec(memory_space=pltpu.HBM)
 SMEM = pl.BlockSpec(memory_space=pltpu.SMEM)
 
 
@@ -70,8 +72,16 @@
 
 
 def prep_kernel(
-    probe, weights, points, skeleton, row_basis, col_basis, near_leaf, send, out, back, own, block, coef_t, feat_t, sk, cnt, pts
+    probe_h, weights_h, points_h, skeleton_h, row_basis_h, col_basis_h, near_leaf_h, send_h, out, back, own, block,
+    probe, weights, points, skeleton, row_basis, col_basis, near_leaf, send, coef_t, feat_t, sk, cnt, pts, sems
 ):
+    far = (near_leaf_h, points_h, skeleton_h, probe_h, weights_h, col_basis_h, row_basis_h, send_h)
+    here = (near_leaf, points, skeleton, probe, weights, col_basis, row_basis, send)
+    copies = [pltpu.make_async_copy(f, h, sems.at[n]) for n, (f, h) in enumerate(zip(far, here))]
+    for copy in copies:
+        copy.start()
+    for copy in copies[:3]:
+        copy.wait()
     low = lax.broadcasted_iota(jnp.int32, (RHS, 128), 1) < RANK
     low8 = lax.broadcasted_iota(jnp.int32, (8, 128), 1) < RANK
     low64 = lax.broadcasted_iota(jnp.int32, (LEAVES, 128), 1) < RANK
@@ -91,6 +101,8 @@
     cnt[...] = jnp.concatenate([total, jnp.zeros((96, 128), f32)], axis=0).T[0:LEAVES]
     for c in range(3):
         pts[c] = points[c].astype(f32)
+    for copy in copies[3:]:
+        copy.wait()
 
     def leaf(j, _):
         c = lax.dot_general(probe[j], col_basis[j], NT, preferred_element_type=f32)
@@ -106,7 +118,7 @@
         block[j, 32:48, :] = stack_rows(rows, 16, SIZE).astype(bf16)
         return 0
 
-    lax.fori_loop(0, LEAVES, leaf, 0, unroll=4)
+    lax.fori_loop(0, LEAVES, leaf, 0, unroll=8)
 
     def peer(d, _):
         at = [send[q, d] for q in range(CAP)]
@@ -116,7 +128,7 @@
         out[d, :, 256:384] = jnp.concatenate(f, axis=0).astype(bf16)
         return 0
 
-    lax.fori_loop(0, PEERS, peer, 0, unroll=4)
+    lax.fori_loop(0, PEERS, peer, 0, unroll=8)
 
 
 def prep(*operands):
@@ -128,16 +140,19 @@
             jax.ShapeDtypeStruct((LEAVES, RANK, 128), bf16),
             jax.ShapeDtypeStruct((LEAVES, ROWS, SIZE), bf16),
         ),
-        in_specs=[VMEM] * 7 + [SMEM],
+        in_specs=[HBM] * 8,
         out_specs=(VMEM,) * 4,
-        scratch_shapes=[
+        scratch_shapes=[pltpu.VMEM(a.shape, a.dtype) for a in operands[:7]]
+        + [
+            pltpu.SMEM((CAP, PEERS), jnp.int32),
             pltpu.VMEM((LEAVES, RHS, 128), bf16),
             pltpu.VMEM((LEAVES, 8, 128), f32),
             pltpu.VMEM((3, LEAVES, 128), f32),
             pltpu.VMEM((LEAVES, 128), f32),
             pltpu.VMEM((3, LEAVES, SIZE), f32),
+            pltpu.SemaphoreType.DMA((8,)),
         ],
-        compiler_params=params(),
+        compiler_params=params(PREP_MIB),
         name="prep",
     )(*operands)
 
@@ -150,7 +165,8 @@
         pl.semaphore_signal(barrier, inc=1, device_id=(peer // 4, lax.rem(peer, 4)), device_id_type=MESH)
         return 0
 
-    lax.fori_loop(1, PEERS, one, 0)
+    one(1, 0)
+    lax.fori_loop(2, PEERS, one, 0, unroll=6)
 
 
 def all_here():
@@ -172,7 +188,8 @@
         ).start()
         return 0
 
-    lax.fori_loop(1, PEERS, one, 0)
+    one(1, 0)
+    lax.fori_loop(2, PEERS, one, 0, unroll=6)
 
 
 def wait_all(me, source, target, send_sem, recv_sem, own_sem):
@@ -336,12 +353,18 @@
 
     lax.fori_loop(0, REACH, edge, 0, unroll=2)
 
-    def first(j, _):
+    def keep(j, _):
+        acc[j + REACH] = before[j]
+        return 0
+
+    lax.fori_loop(0, LEAVES, keep, 0, unroll=4)
+
+    def first(n, _):
+        j = jnp.where(n < REACH, n, n - REACH + FIRST_COLUMNS)
         near.features(j + REACH, block[j])
-        acc[j + REACH] = before[j]
-        return 0
-
-    lax.fori_loop(0, LEAVES, first, 0, unroll=4)
+        return 0
+
+    lax.fori_loop(0, REACH + LEAVES - FIRST_COLUMNS, first, 0, unroll=4)
     begin = 2 * REACH + FIRST_COLUMNS
     upper = EXT - begin
     columns = upper + REACH
@@ -451,12 +474,12 @@
     def pack(d, _):
         for h in range(2):
             s = d * CAP + 2 * h
-            even = acc_l[s] + pltpu.roll(acc_u[s], RANK, 1)
-            odd = pltpu.roll(acc_l[s + 1], RANK, 1) + acc_u[s + 1]
-            ret[d, :, h * 128 : (h + 1) * 128] = jnp.where(low, even, odd).astype(bf16)
-        return 0
-
-    lax.fori_loop(0, PEERS, pack, 0, unroll=4)
+            here = jnp.where(low, acc_l[s], acc_u[s + 1])
+            over = jnp.where(low, acc_l[s + 1], acc_u[s])
+            ret[d, :, h * 128 : (h + 1) * 128] = (here + pltpu.roll(over, RANK, 1)).astype(bf16)
+        return 0
+
+    lax.fori_loop(0, PEERS, pack, 0, unroll=8)
 
 
 def far(arrived, own, back, slot):
@@ -496,7 +519,7 @@
             acc_u[send[2 * h + 1, d]] += tile
         return 0
 
-    lax.fori_loop(0, PEERS, peer, 0, unroll=4)
+    lax.fori_loop(0, PEERS, peer, 0, unroll=8)
 
     def leaf(j, _):
         total = (acc_l[j] + pltpu.roll(acc_u[j], RANK, 1))[:, :RANK].astype(bf16)
@@ -504,7 +527,7 @@
         product[j] = near_out[j, :RHS, :] + jnp.dot(far_in[j], row_basis[j], preferred_element_type=f32)
         return 0
 
-    lax.fori_loop(0, LEAVES, leaf, 0, unroll=4)
+    lax.fori_loop(0, LEAVES, leaf, 0, unroll=8)
 
 
 def post(came, send, near_out, far_in, row_basis, col_basis):

time: 143 us -> 132 us (0.923)
  Pallas kernels: 134 us -> 128 us
  local copies, waits for them, and re-layouts: 8.31 us -> 2.84 us
    pallas_call x1, Pallas kernels: 46.5 us -> 33.5 us  [near_rest(): pl.pallas_call(near_rest_kernel, out_shape=(jax.ShapeDtypeStruct((LEAVES,...]
    pallas_call x1, Pallas kernels: 37.2 us -> 45.6 us  [near_first(): pl.pallas_call(near_first_kernel, out_shape=(jax.ShapeDtypeStruct((LEAVES...]
    unnamed x24 -> x18, local copies, waits for them, and re-layouts: 8.31 us -> 2.84 us
    pallas_call x1, Pallas kernels: 6.24 us -> 8.55 us  [prep(): pl.pallas_call(prep_kernel, out_shape=(jax.ShapeDtypeStruct((PEERS, RHS,...]
    pallas_call x1, Pallas kernels: 37.3 us -> 35.5 us  [far(): pl.pallas_call(far_kernel, out_shape=(jax.ShapeDtypeStruct((LEAVES, RHS,...]
    pallas_call x1, Pallas kernels: 6.61 us -> 5.09 us  [post(): pl.pallas_call(post_kernel, out_shape=(jax.ShapeDtypeStruct((LEAVES, RHS,...]
where the time goes in v4:
time: 132 us
  Pallas kernels  128 us (97%)
  local copies, waits for them, and re-layouts  2.84 us (2%)
    pallas_call x1, Pallas kernels, near_first(): pl.pallas_call(near_first_kernel, out_shape=(jax.ShapeDtypeStruct((LEAVES...  45.6 us
    pallas_call x1, Pallas kernels, far(): pl.pallas_call(far_kernel, out_shape=(jax.ShapeDtypeStruct((LEAVES, RHS,...  35.5 us
    pallas_call x1, Pallas kernels, near_rest(): pl.pallas_call(near_rest_kernel, out_shape=(jax.ShapeDtypeStruct((LEAVES,...  33.5 us
    pallas_call x1, Pallas kernels, prep(): pl.pallas_call(prep_kernel, out_shape=(jax.ShapeDtypeStruct((PEERS, RHS,...  8.55 us
    pallas_call x1, Pallas kernels, post(): pl.pallas_call(post_kernel, out_shape=(jax.ShapeDtypeStruct((LEAVES, RHS,...  5.09 us
    unnamed x18, local copies, waits for them, and re-layouts  2.84 us

profile of v4, /device:TPU:1, one launch (start us, length us, event | category | flops | bytes accessed | tf_op | source)
XLA Modules:
  0.0 131.8 jit_solution(5127009944230072315)
XLA Ops:
  0.6 8.6 %prep.1 = (bf16[128,16,384]{2,1,0:T(8,128)(2,1)}, bf16[64,16,64]{2,1,0:T(8,128)(2,1)}, bf16[64,64,128]{2,1,0:T(8,128)(2,1)}, bf16[64,48,256]{2,1,0:T(8,128)(2,1)}) custom-call(bf16[64,16,256]{2,1,0:T(8,128)(2,1)} %probe_h.1, bf16[64,16,256]{2,1,0:T(8,128)(2,1)} %weights_h.1, bf16[3,64,256]{2,1,0:T(8,128)(2,1)} %bitcast.7, bf16[64,192]{1,0:T(8,128)(2,1)} %skeleton_h.1, ...), custom_call_target="tpu_custom_call" | custom-call | tf_op jit(solution)/shard_map/prep/pallas_call | solution.py:135
  9.2 0.0 copy-start
  9.2 1.4 %copy-done = bf16[64,48,256]{2,1,0:T(8,128)(2,1)S(1)} copy-done((bf16[64,48,256]{2,1,0:T(8,128)(2,1)S(1)}, bf16[64,48,256]{2,1,0:T(8,128)(2,1)}, u32[]{:S(2)}) %copy-start) | copy-done | bytes 1572888
  10.6 0.0 copy-start.4
  10.6 1.4 %copy-done.4 = bf16[128,16,384]{2,1,0:T(8,128)(2,1)S(1)} copy-done((bf16[128,16,384]{2,1,0:T(8,128)(2,1)S(1)}, bf16[128,16,384]{2,1,0:T(8,128)(2,1)}, u32[]{:S(2)}) %copy-start.4) | copy-done | bytes 1572888
  12.0 0.0 copy-start.5
  12.0 0.0 copy-start.6
  12.0 0.0 copy-start.7
  12.0 45.6 %near_first.1 = (f32[64,32,256]{2,1,0:T(8,128)S(1)}, bf16[128,16,384]{2,1,0:T(8,128)(2,1)S(1)}, bf16[16,48,256]{2,1,0:T(8,128)(2,1)S(1)}) custom-call(bf16[64,48,256]{2,1,0:T(8,128)(2,1)S(1)} %copy-done, bf16[128,16,384]{2,1,0:T(8,128)(2,1)S(1)} %copy-done.4, bf16[64,48,256]{2,1,0:T(8,128)(2,1)S(1)} %copy-done), custom_call_target="tpu_custom_call" | custom-call | tf_op jit(solution)/shard_map/near_first/pallas_call | solution.py:322
  57.6 0.0 copy-start.1
  57.6 0.0 copy-done.5
  57.6 0.0 copy-done.6
  57.6 0.0 copy-done.7
  57.7 35.5 %far.1 = (bf16[64,16,64]{2,1,0:T(8,128)(2,1)S(1)}, bf16[128,16,256]{2,1,0:T(8,128)(2,1)S(1)}) custom-call(bf16[128,16,384]{2,1,0:T(8,128)(2,1)S(1)} %get-tuple-element.17.arrived, bf16[64,64,128]{2,1,0:T(8,128)(2,1)S(1)} %copy-done.5, bf16[64,16,64]{2,1,0:T(8,128)(2,1)S(1)} %copy-done.6, s32[64,64]{1,0:T(8,128)S(1)} %copy-done.7), custom_call_target="tpu_custom_call" | custom-call | tf_op jit(solution)/shard_map/far/pallas_call | solution.py:486
  93.1 0.0 copy-done.1
  93.1 0.0 copy-start.2
  93.2 0.0 copy-start.3
  93.2 0.0 copy-start.8
  93.2 33.5 %near_rest.1 = (f32[64,32,256]{2,1,0:T(8,128)S(1)}, bf16[128,16,256]{2,1,0:T(8,128)(2,1)S(1)}) custom-call(bf16[64,48,256]{2,1,0:T(8,128)(2,1)S(1)} %copy-done.1, bf16[16,48,256]{2,1,0:T(8,128)(2,1)S(1)} %get-tuple-element.15.halo, f32[64,32,256]{2,1,0:T(8,128)S(1)} %get-tuple-element.16.before, bf16[128,16,256]{2,1,0:T(8,128)(2,1)S(1)} %get-tuple-element.20.ret), custom_call_target="tpu_custom_call" | custom-call | tf_op jit(solution)/shard_map/near_rest/pallas_call | solution.py:392
  126.7 0.0 copy-done.2
  126.7 0.0 copy-done.3
  126.7 0.0 copy-done.8
  126.8 5.1 %post.1 = (f32[64,16,256]{2,1,0:T(8,128)}, f32[64,16,256]{2,1,0:T(8,128)}) custom-call(bf16[128,16,256]{2,1,0:T(8,128)(2,1)S(1)} %get-tuple-element.21.came, s32[4,128]{1,0:T(4,128)S(1)} %bitcast.6, f32[64,32,256]{2,1,0:T(8,128)S(1)} %get-tuple-element.22.near_out, bf16[64,16,64]{2,1,0:T(8,128)(2,1)S(1)} %get-tuple-element.23.far_in, ...), custom_call_target="tpu_custom_call" | custom-call | tf_op jit(solution)/shard_map/post/pallas_call | solution.py:534
Async XLA Ops:
  9.2 1.4 %copy-start = (bf16[64,48,256]{2,1,0:T(8,128)(2,1)S(1)}, bf16[64,48,256]{2,1,0:T(8,128)(2,1)}, u32[]{:S(2)}) copy-start(bf16[64,48,256]{2,1,0:T(8,128)(2,1)} %get-tuple-element.13.block.block_far) | copy-start | bytes 4718596
  10.6 1.4 %copy-start.4 = (bf16[128,16,384]{2,1,0:T(8,128)(2,1)S(1)}, bf16[128,16,384]{2,1,0:T(8,128)(2,1)}, u32[]{:S(2)}) copy-start(bf16[128,16,384]{2,1,0:T(8,128)(2,1)} %get-tuple-element.14.payload) | copy-start | bytes 4718596
  12.0 45.6 %copy-start.5 = (bf16[64,64,128]{2,1,0:T(8,128)(2,1)S(1)}, bf16[64,64,128]{2,1,0:T(8,128)(2,1)}, u32[]{:S(2)}) copy-start(bf16[64,64,128]{2,1,0:T(8,128)(2,1)} %get-tuple-element.18.own) | copy-start | bytes 3145732
  12.0 45.6 %copy-start.6 = (bf16[64,16,64]{2,1,0:T(8,128)(2,1)S(1)}, bf16[64,16,64]{2,1,0:T(8,128)(2,1)}, u32[]{:S(2)}) copy-start(bf16[64,16,64]{2,1,0:T(8,128)(2,1)} %get-tuple-element.19.back) | copy-start | bytes 393220
  12.0 45.6 %copy-start.7 = (s32[64,64]{1,0:T(8,128)S(1)}, s32[64,64]{1,0:T(8,128)}, u32[]{:S(2)}) copy-start(s32[64,64]{1,0:T(8,128)} %slot.1) | copy-start | bytes 49156
  57.6 35.5 %copy-start.1 = (bf16[64,48,256]{2,1,0:T(8,128)(2,1)S(1)}, bf16[64,48,256]{2,1,0:T(8,128)(2,1)}, u32[]{:S(2)}) copy-start(bf16[64,48,256]{2,1,0:T(8,128)(2,1)} %get-tuple-element.13.block.block_far) | copy-start | bytes 4718596
  93.1 33.6 %copy-start.2 = (bf16[64,64,256]{2,1,0:T(8,128)(2,1)S(1)}, bf16[64,64,256]{2,1,0:T(8,128)(2,1)}, u32[]{:S(2)}) copy-start(bf16[64,64,256]{2,1,0:T(8,128)(2,1)} %row_basis.1) | copy-start | bytes 6291460
  93.2 33.6 %copy-start.3 = (bf16[64,64,256]{2,1,0:T(8,128)(2,1)S(1)}, bf16[64,64,256]{2,1,0:T(8,128)(2,1)}, u32[]{:S(2)}) copy-start(bf16[64,64,256]{2,1,0:T(8,128)(2,1)} %col_basis.1) | copy-start | bytes 6291460
  93.2 33.6 %copy-start.8 = (s32[1,128,4]{1,2,0:T(4,128)S(1)}, s32[1,128,4]{1,2,0:T(4,128)}, u32[]{:S(2)}) copy-start(s32[1,128,4]{1,2,0:T(4,128)} %param.17) | copy-start | bytes 6148

commit v5 on v4

--- a/solution.py
+++ b/solution.py
@@ -29,6 +29,7 @@
 MESH = pl.DeviceIdType.MESH
 ROWS = 48
 FIRST_COLUMNS = 40
+LAG = 4
 VMEM = pl.BlockSpec(memory_space=pltpu.VMEM)
 ANY = pl.BlockSpec(memory_space=pl.ANY)
 HBM = pl.BlockSpec(memory_space=pltpu.HBM)
@@ -253,6 +254,38 @@
         acc[j] += total
 
 
+    def upper_edge(self, g):
+        lane = lax.broadcasted_iota(jnp.int32, (1, 128), 1)
+        kt, acc = self.kt[0], self.acc
+
+        def pick(row, at):
+            c = jnp.sum(jnp.where(lane == at, row, 0.0), axis=1, keepdims=True)
+            c = jnp.broadcast_to(c, (RHS, 128))
+            return jnp.concatenate([c, c], axis=1).astype(bf16)
+
+        def make(b, i, j):
+            v = jnp.dot(self.left_t[i, :, 0:16], self.right_t[j], preferred_element_type=f32)
+            kt[b * SIZE : (b + 1) * SIZE, :] = kappa(v).T
+
+        def apply(b, i, j, d):
+            ahead = pick(self.cnt[i], REACH + d)
+            behind = pick(self.cnt[j], REACH - d)
+            vj = self.vec[j]
+            vb = jnp.concatenate([vj[0:16] * ahead, vj[16:32] * behind], axis=0)
+            acc[i] += jnp.dot(vb, kt[b * SIZE : (b + 1) * SIZE, :], preferred_element_type=f32)
+
+        pairs = []
+        for b in range(BAND + LAG):
+            if b < BAND:
+                one = b < REACH - g
+                i = jnp.where(one, LEAVES + g + b, LEAVES + b - 1)
+                j = jnp.where(one, LEAVES + REACH + g, EXT - 1 - g)
+                pairs.append((i, j, jnp.where(one, REACH - b, 2 * REACH - b - g)))
+                make(b, i, j)
+            if b >= LAG:
+                apply(b - LAG, *pairs[b - LAG])
+
+
 NEAR_SCRATCH = [
     pltpu.VMEM((EXT, 2 * RHS, SIZE), bf16),
     pltpu.VMEM((EXT, 1, 128), f32),
@@ -366,7 +399,7 @@
 
     lax.fori_loop(0, REACH + LEAVES - FIRST_COLUMNS, first, 0, unroll=4)
     begin = 2 * REACH + FIRST_COLUMNS
-    upper = EXT - begin
+    upper = LEAVES + REACH - begin
     columns = upper + REACH
 
     def column(n):
@@ -384,6 +417,12 @@
     lax.fori_loop(0, columns // 2 - 1, body, 0)
     near.step(column(columns - 2), 0, column(columns - 1))
     near.step(column(columns - 1), 1)
+
+    def last(g, _):
+        near.upper_edge(g)
+        return 0
+
+    lax.fori_loop(0, REACH // 2, last, 0)
     out[...] = acc[REACH : REACH + LEAVES]
     wait_all(me, ret, came, send_sem, recv_sem, own_sem)
 

time: 132 us -> 129 us (0.977)
  Pallas kernels: 128 us -> 126 us
    pallas_call x1, Pallas kernels: 33.5 us -> 31.2 us  [near_rest(): pl.pallas_call(near_rest_kernel, out_shape=(jax.ShapeDtypeStruct((LEAVES,...]
where the time goes in v5:
time: 129 us
  Pallas kernels  126 us (98%)
  local copies, waits for them, and re-layouts  2.84 us (2%)
    pallas_call x1, Pallas kernels, near_first(): pl.pallas_call(near_first_kernel, out_shape=(jax.ShapeDtypeStruct((LEAVES...  45.6 us
    pallas_call x1, Pallas kernels, far(): pl.pallas_call(far_kernel, out_shape=(jax.ShapeDtypeStruct((LEAVES, RHS,...  35.3 us
    pallas_call x1, Pallas kernels, near_rest(): pl.pallas_call(near_rest_kernel, out_shape=(jax.ShapeDtypeStruct((LEAVES,...  31.2 us
    pallas_call x1, Pallas kernels, prep(): pl.pallas_call(prep_kernel, out_shape=(jax.ShapeDtypeStruct((PEERS, RHS,...  8.55 us
    pallas_call x1, Pallas kernels, post(): pl.pallas_call(post_kernel, out_shape=(jax.ShapeDtypeStruct((LEAVES, RHS,...  5.08 us
    unnamed x18, local copies, waits for them, and re-layouts  2.84 us

profile of v5, /device:TPU:1, one launch (start us, length us, event | category | flops | bytes accessed | tf_op | source)
XLA Modules:
  0.0 129.3 jit_solution(6766230916979261020)
XLA Ops:
  0.6 8.6 %prep.1 = (bf16[128,16,384]{2,1,0:T(8,128)(2,1)}, bf16[64,16,64]{2,1,0:T(8,128)(2,1)}, bf16[64,64,128]{2,1,0:T(8,128)(2,1)}, bf16[64,48,256]{2,1,0:T(8,128)(2,1)}) custom-call(bf16[64,16,256]{2,1,0:T(8,128)(2,1)} %probe_h.1, bf16[64,16,256]{2,1,0:T(8,128)(2,1)} %weights_h.1, bf16[3,64,256]{2,1,0:T(8,128)(2,1)} %bitcast.7, bf16[64,192]{1,0:T(8,128)(2,1)} %skeleton_h.1, ...), custom_call_target="tpu_custom_call" | custom-call | tf_op jit(solution)/shard_map/prep/pallas_call | solution.py:136
  9.2 0.0 copy-start
  9.2 1.4 %copy-done = bf16[64,48,256]{2,1,0:T(8,128)(2,1)S(1)} copy-done((bf16[64,48,256]{2,1,0:T(8,128)(2,1)S(1)}, bf16[64,48,256]{2,1,0:T(8,128)(2,1)}, u32[]{:S(2)}) %copy-start) | copy-done | bytes 1572888
  10.6 0.0 copy-start.4
  10.6 1.4 %copy-done.4 = bf16[128,16,384]{2,1,0:T(8,128)(2,1)S(1)} copy-done((bf16[128,16,384]{2,1,0:T(8,128)(2,1)S(1)}, bf16[128,16,384]{2,1,0:T(8,128)(2,1)}, u32[]{:S(2)}) %copy-start.4) | copy-done | bytes 1572888
  12.0 0.0 copy-start.5
  12.0 0.0 copy-start.6
  12.0 0.0 copy-start.7
  12.0 45.6 %near_first.1 = (f32[64,32,256]{2,1,0:T(8,128)S(1)}, bf16[128,16,384]{2,1,0:T(8,128)(2,1)S(1)}, bf16[16,48,256]{2,1,0:T(8,128)(2,1)S(1)}) custom-call(bf16[64,48,256]{2,1,0:T(8,128)(2,1)S(1)} %copy-done, bf16[128,16,384]{2,1,0:T(8,128)(2,1)S(1)} %copy-done.4, bf16[64,48,256]{2,1,0:T(8,128)(2,1)S(1)} %copy-done), custom_call_target="tpu_custom_call" | custom-call | tf_op jit(solution)/shard_map/near_first/pallas_call | solution.py:355
  57.6 0.0 copy-start.1
  57.6 0.0 copy-done.5
  57.6 0.0 copy-done.6
  57.6 0.0 copy-done.7
  57.7 35.3 %far.1 = (bf16[64,16,64]{2,1,0:T(8,128)(2,1)S(1)}, bf16[128,16,256]{2,1,0:T(8,128)(2,1)S(1)}) custom-call(bf16[128,16,384]{2,1,0:T(8,128)(2,1)S(1)} %get-tuple-element.17.arrived, bf16[64,64,128]{2,1,0:T(8,128)(2,1)S(1)} %copy-done.5, bf16[64,16,64]{2,1,0:T(8,128)(2,1)S(1)} %copy-done.6, s32[64,64]{1,0:T(8,128)S(1)} %copy-done.7), custom_call_target="tpu_custom_call" | custom-call | tf_op jit(solution)/shard_map/far/pallas_call | solution.py:525
  93.0 0.0 copy-done.1
  93.0 0.0 copy-start.2
  93.0 0.0 copy-start.3
  93.0 0.0 copy-start.8
  93.0 31.2 %near_rest.1 = (f32[64,32,256]{2,1,0:T(8,128)S(1)}, bf16[128,16,256]{2,1,0:T(8,128)(2,1)S(1)}) custom-call(bf16[64,48,256]{2,1,0:T(8,128)(2,1)S(1)} %copy-done.1, bf16[16,48,256]{2,1,0:T(8,128)(2,1)S(1)} %get-tuple-element.15.halo, f32[64,32,256]{2,1,0:T(8,128)S(1)} %get-tuple-element.16.before, bf16[128,16,256]{2,1,0:T(8,128)(2,1)S(1)} %get-tuple-element.20.ret), custom_call_target="tpu_custom_call" | custom-call | tf_op jit(solution)/shard_map/near_rest/pallas_call | solution.py:431
  124.2 0.0 copy-done.2
  124.2 0.0 copy-done.3
  124.2 0.0 copy-done.8
  124.2 5.1 %post.1 = (f32[64,16,256]{2,1,0:T(8,128)}, f32[64,16,256]{2,1,0:T(8,128)}) custom-call(bf16[128,16,256]{2,1,0:T(8,128)(2,1)S(1)} %get-tuple-element.21.came, s32[4,128]{1,0:T(4,128)S(1)} %bitcast.6, f32[64,32,256]{2,1,0:T(8,128)S(1)} %get-tuple-element.22.near_out, bf16[64,16,64]{2,1,0:T(8,128)(2,1)S(1)} %get-tuple-element.23.far_in, ...), custom_call_target="tpu_custom_call" | custom-call | tf_op jit(solution)/shard_map/post/pallas_call | solution.py:573
Async XLA Ops:
  9.2 1.4 %copy-start = (bf16[64,48,256]{2,1,0:T(8,128)(2,1)S(1)}, bf16[64,48,256]{2,1,0:T(8,128)(2,1)}, u32[]{:S(2)}) copy-start(bf16[64,48,256]{2,1,0:T(8,128)(2,1)} %get-tuple-element.13.block.block_far) | copy-start | bytes 4718596
  10.6 1.4 %copy-start.4 = (bf16[128,16,384]{2,1,0:T(8,128)(2,1)S(1)}, bf16[128,16,384]{2,1,0:T(8,128)(2,1)}, u32[]{:S(2)}) copy-start(bf16[128,16,384]{2,1,0:T(8,128)(2,1)} %get-tuple-element.14.payload) | copy-start | bytes 4718596
  12.0 45.6 %copy-start.5 = (bf16[64,64,128]{2,1,0:T(8,128)(2,1)S(1)}, bf16[64,64,128]{2,1,0:T(8,128)(2,1)}, u32[]{:S(2)}) copy-start(bf16[64,64,128]{2,1,0:T(8,128)(2,1)} %get-tuple-element.18.own) | copy-start | bytes 3145732
  12.0 45.6 %copy-start.6 = (bf16[64,16,64]{2,1,0:T(8,128)(2,1)S(1)}, bf16[64,16,64]{2,1,0:T(8,128)(2,1)}, u32[]{:S(2)}) copy-start(bf16[64,16,64]{2,1,0:T(8,128)(2,1)} %get-tuple-element.19.back) | copy-start | bytes 393220
  12.0 45.6 %copy-start.7 = (s32[64,64]{1,0:T(8,128)S(1)}, s32[64,64]{1,0:T(8,128)}, u32[]{:S(2)}) copy-start(s32[64,64]{1,0:T(8,128)} %slot.1) | copy-start | bytes 49156
  57.6 35.4 %copy-start.1 = (bf16[64,48,256]{2,1,0:T(8,128)(2,1)S(1)}, bf16[64,48,256]{2,1,0:T(8,128)(2,1)}, u32[]{:S(2)}) copy-start(bf16[64,48,256]{2,1,0:T(8,128)(2,1)} %get-tuple-element.13.block.block_far) | copy-start | bytes 4718596
  93.0 31.2 %copy-start.2 = (bf16[64,64,256]{2,1,0:T(8,128)(2,1)S(1)}, bf16[64,64,256]{2,1,0:T(8,128)(2,1)}, u32[]{:S(2)}) copy-start(bf16[64,64,256]{2,1,0:T(8,128)(2,1)} %row_basis.1) | copy-start | bytes 6291460
  93.0 31.2 %copy-start.3 = (bf16[64,64,256]{2,1,0:T(8,128)(2,1)S(1)}, bf16[64,64,256]{2,1,0:T(8,128)(2,1)}, u32[]{:S(2)}) copy-start(bf16[64,64,256]{2,1,0:T(8,128)(2,1)} %col_basis.1) | copy-start | bytes 6291460
  93.0 31.2 %copy-start.8 = (s32[1,128,4]{1,2,0:T(4,128)S(1)}, s32[1,128,4]{1,2,0:T(4,128)}, u32[]{:S(2)}) copy-start(s32[1,128,4]{1,2,0:T(4,128)} %param.17) | copy-start | bytes 6148

commit v6 on v5

--- a/solution.py
+++ b/solution.py
@@ -45,8 +45,8 @@
 
 
 def kappa(v):
-    s = v * lax.rsqrt(v)
-    return ((s * (0.5 * SCALE) + 0.5) * jnp.exp2(s * (-SCALE * LOG2E))).astype(bf16)
+    z = (v * lax.rsqrt(v) * (-SCALE * LOG2E)).astype(bf16)
+    return (bf16(0.5) - z * bf16(0.5 / LOG2E)) * jnp.exp2(z)
 
 
 def split3(n):

time: 129 us -> 128 us (level)
  no operation moved by 1% of the time
where the time goes in v6:
time: 128 us
  Pallas kernels  125 us (98%)
  local copies, waits for them, and re-layouts  2.84 us (2%)
    pallas_call x1, Pallas kernels, near_first(): pl.pallas_call(near_first_kernel, out_shape=(jax.ShapeDtypeStruct((LEAVES...  45 us
    pallas_call x1, Pallas kernels, far(): pl.pallas_call(far_kernel, out_shape=(jax.ShapeDtypeStruct((LEAVES, RHS,...  35.8 us
    pallas_call x1, Pallas kernels, near_rest(): pl.pallas_call(near_rest_kernel, out_shape=(jax.ShapeDtypeStruct((LEAVES,...  30.1 us
    pallas_call x1, Pallas kernels, prep(): pl.pallas_call(prep_kernel, out_shape=(jax.ShapeDtypeStruct((PEERS, RHS,...  8.55 us
    pallas_call x1, Pallas kernels, post(): pl.pallas_call(post_kernel, out_shape=(jax.ShapeDtypeStruct((LEAVES, RHS,...  5.08 us
    unnamed x18, local copies, waits for them, and re-layouts  2.84 us

profile of v6, /device:TPU:1, one launch (start us, length us, event | category | flops | bytes accessed | tf_op | source)
XLA Modules:
  0.0 128.1 jit_solution(13728051641029722568)
XLA Ops:
  0.6 8.6 %prep.1 = (bf16[128,16,384]{2,1,0:T(8,128)(2,1)}, bf16[64,16,64]{2,1,0:T(8,128)(2,1)}, bf16[64,64,128]{2,1,0:T(8,128)(2,1)}, bf16[64,48,256]{2,1,0:T(8,128)(2,1)}) custom-call(bf16[64,16,256]{2,1,0:T(8,128)(2,1)} %probe_h.1, bf16[64,16,256]{2,1,0:T(8,128)(2,1)} %weights_h.1, bf16[3,64,256]{2,1,0:T(8,128)(2,1)} %bitcast.7, bf16[64,192]{1,0:T(8,128)(2,1)} %skeleton_h.1, ...), custom_call_target="tpu_custom_call" | custom-call | tf_op jit(solution)/shard_map/prep/pallas_call | solution.py:136
  9.2 0.0 copy-start
  9.2 1.4 %copy-done = bf16[64,48,256]{2,1,0:T(8,128)(2,1)S(1)} copy-done((bf16[64,48,256]{2,1,0:T(8,128)(2,1)S(1)}, bf16[64,48,256]{2,1,0:T(8,128)(2,1)}, u32[]{:S(2)}) %copy-start) | copy-done | bytes 1572888
  10.6 0.0 copy-start.4
  10.6 1.4 %copy-done.4 = bf16[128,16,384]{2,1,0:T(8,128)(2,1)S(1)} copy-done((bf16[128,16,384]{2,1,0:T(8,128)(2,1)S(1)}, bf16[128,16,384]{2,1,0:T(8,128)(2,1)}, u32[]{:S(2)}) %copy-start.4) | copy-done | bytes 1572888
  12.0 0.0 copy-start.5
  12.0 0.0 copy-start.6
  12.0 0.0 copy-start.7
  12.0 45.0 %near_first.1 = (f32[64,32,256]{2,1,0:T(8,128)S(1)}, bf16[128,16,384]{2,1,0:T(8,128)(2,1)S(1)}, bf16[16,48,256]{2,1,0:T(8,128)(2,1)S(1)}) custom-call(bf16[64,48,256]{2,1,0:T(8,128)(2,1)S(1)} %copy-done, bf16[128,16,384]{2,1,0:T(8,128)(2,1)S(1)} %copy-done.4, bf16[64,48,256]{2,1,0:T(8,128)(2,1)S(1)} %copy-done), custom_call_target="tpu_custom_call" | custom-call | tf_op jit(solution)/shard_map/near_first/pallas_call | solution.py:355
  57.0 0.0 copy-start.1
  57.1 0.0 copy-done.5
  57.1 0.0 copy-done.6
  57.1 0.0 copy-done.7
  57.1 35.8 %far.1 = (bf16[64,16,64]{2,1,0:T(8,128)(2,1)S(1)}, bf16[128,16,256]{2,1,0:T(8,128)(2,1)S(1)}) custom-call(bf16[128,16,384]{2,1,0:T(8,128)(2,1)S(1)} %get-tuple-element.17.arrived, bf16[64,64,128]{2,1,0:T(8,128)(2,1)S(1)} %copy-done.5, bf16[64,16,64]{2,1,0:T(8,128)(2,1)S(1)} %copy-done.6, s32[64,64]{1,0:T(8,128)S(1)} %copy-done.7), custom_call_target="tpu_custom_call" | custom-call | tf_op jit(solution)/shard_map/far/pallas_call | solution.py:525
  92.9 0.0 copy-done.1
  92.9 0.0 copy-start.2
  92.9 0.0 copy-start.3
  92.9 0.0 copy-start.8
  92.9 30.1 %near_rest.1 = (f32[64,32,256]{2,1,0:T(8,128)S(1)}, bf16[128,16,256]{2,1,0:T(8,128)(2,1)S(1)}) custom-call(bf16[64,48,256]{2,1,0:T(8,128)(2,1)S(1)} %copy-done.1, bf16[16,48,256]{2,1,0:T(8,128)(2,1)S(1)} %get-tuple-element.15.halo, f32[64,32,256]{2,1,0:T(8,128)S(1)} %get-tuple-element.16.before, bf16[128,16,256]{2,1,0:T(8,128)(2,1)S(1)} %get-tuple-element.20.ret), custom_call_target="tpu_custom_call" | custom-call | tf_op jit(solution)/shard_map/near_rest/pallas_call | solution.py:431
  123.0 0.0 copy-done.2
  123.0 0.0 copy-done.3
  123.1 0.0 copy-done.8
  123.1 5.1 %post.1 = (f32[64,16,256]{2,1,0:T(8,128)}, f32[64,16,256]{2,1,0:T(8,128)}) custom-call(bf16[128,16,256]{2,1,0:T(8,128)(2,1)S(1)} %get-tuple-element.21.came, s32[4,128]{1,0:T(4,128)S(1)} %bitcast.6, f32[64,32,256]{2,1,0:T(8,128)S(1)} %get-tuple-element.22.near_out, bf16[64,16,64]{2,1,0:T(8,128)(2,1)S(1)} %get-tuple-element.23.far_in, ...), custom_call_target="tpu_custom_call" | custom-call | tf_op jit(solution)/shard_map/post/pallas_call | solution.py:573
Async XLA Ops:
  9.2 1.4 %copy-start = (bf16[64,48,256]{2,1,0:T(8,128)(2,1)S(1)}, bf16[64,48,256]{2,1,0:T(8,128)(2,1)}, u32[]{:S(2)}) copy-start(bf16[64,48,256]{2,1,0:T(8,128)(2,1)} %get-tuple-element.13.block.block_far) | copy-start | bytes 4718596
  10.6 1.4 %copy-start.4 = (bf16[128,16,384]{2,1,0:T(8,128)(2,1)S(1)}, bf16[128,16,384]{2,1,0:T(8,128)(2,1)}, u32[]{:S(2)}) copy-start(bf16[128,16,384]{2,1,0:T(8,128)(2,1)} %get-tuple-element.14.payload) | copy-start | bytes 4718596
  12.0 45.0 %copy-start.5 = (bf16[64,64,128]{2,1,0:T(8,128)(2,1)S(1)}, bf16[64,64,128]{2,1,0:T(8,128)(2,1)}, u32[]{:S(2)}) copy-start(bf16[64,64,128]{2,1,0:T(8,128)(2,1)} %get-tuple-element.18.own) | copy-start | bytes 3145732
  12.0 45.1 %copy-start.6 = (bf16[64,16,64]{2,1,0:T(8,128)(2,1)S(1)}, bf16[64,16,64]{2,1,0:T(8,128)(2,1)}, u32[]{:S(2)}) copy-start(bf16[64,16,64]{2,1,0:T(8,128)(2,1)} %get-tuple-element.19.back) | copy-start | bytes 393220
  12.0 45.1 %copy-start.7 = (s32[64,64]{1,0:T(8,128)S(1)}, s32[64,64]{1,0:T(8,128)}, u32[]{:S(2)}) copy-start(s32[64,64]{1,0:T(8,128)} %slot.1) | copy-start | bytes 49156
  57.0 35.8 %copy-start.1 = (bf16[64,48,256]{2,1,0:T(8,128)(2,1)S(1)}, bf16[64,48,256]{2,1,0:T(8,128)(2,1)}, u32[]{:S(2)}) copy-start(bf16[64,48,256]{2,1,0:T(8,128)(2,1)} %get-tuple-element.13.block.block_far) | copy-start | bytes 4718596
  92.9 30.2 %copy-start.2 = (bf16[64,64,256]{2,1,0:T(8,128)(2,1)S(1)}, bf16[64,64,256]{2,1,0:T(8,128)(2,1)}, u32[]{:S(2)}) copy-start(bf16[64,64,256]{2,1,0:T(8,128)(2,1)} %row_basis.1) | copy-start | bytes 6291460
  92.9 30.2 %copy-start.3 = (bf16[64,64,256]{2,1,0:T(8,128)(2,1)S(1)}, bf16[64,64,256]{2,1,0:T(8,128)(2,1)}, u32[]{:S(2)}) copy-start(bf16[64,64,256]{2,1,0:T(8,128)(2,1)} %col_basis.1) | copy-start | bytes 6291460
  92.9 30.2 %copy-start.8 = (s32[1,128,4]{1,2,0:T(4,128)S(1)}, s32[1,128,4]{1,2,0:T(4,128)}, u32[]{:S(2)}) copy-start(s32[1,128,4]{1,2,0:T(4,128)} %param.17) | copy-start | bytes 6148
